TPU v7x, 32 devices: a whole 2x2x4 slice. The times are simulated.
32 devices in a mesh: groups: 2 (over y), row: 4 (over z), col: 2 (over x), mode: 2 (over core).
Axes of the slice: x: 2, y: 2, z: 4, core: 2. Of those that a mesh axis runs over, the one named last changes fastest.
Arguments:
- object_field: float32 [2048, 2, 1024], P(('groups', 'row'), None, 'col'), parts along dimension 0, may hold values from -12 to 12
- probe_field: float32 [512, 2, 256], P('groups'), parts along dimension 0, may hold values from -5 to 5
- amplitudes: bfloat16 [128, 256, 256], P(('groups', 'row', 'col', 'mode')), parts along dimension 0
- row_offset: int32 [128], P(('groups', 'row', 'col', 'mode')), parts along dimension 0, may hold values from 0 to 768, as said below
- col_offset: int32 [128], P(('groups', 'row', 'col', 'mode')), parts along dimension 0, may hold values from 0 to 768, as said below
- counts: int32 [32], P(('groups', 'row', 'col', 'mode')), parts along dimension 0, may hold values from 1 to 4
Outputs:
- object_new: float32 [2048, 2, 1024], P(('groups', 'row', 'mode'), None, 'col'), parts along dimension 0
- probe_new: float32 [512, 2, 256], P('groups'), parts along dimension 0
There are 2 independent parts, one for each index of `groups`. A program takes and returns all parts, laid end to end along the dimension named above; each array names one. Nothing has to cross between parts.
Inputs may be any that keep to these rules, and one draw needn't show every extreme that they name: `row_offset`: slot j lies on device j div 4 of row+col+mode; its patch starts inside that device's object tile of 256 rows, on a multiple of 64, and stays inside the object. `col_offset`: its patch starts inside the device's tile of 512 columns, on a multiple of 64, and stays inside the object.
All inputs are finite; a program needn't handle non-finite values.
Results may differ from a plain program's by a relative error of at most 0.0007.
The roundings to bfloat16 on the way count: a program that leaves them out, or rounds other values in their place, can miss the bound.
Values may be sent and summed in bfloat16 or wider, within the bound.
No kernel may reach another device: no remote copies, remote signals or barrier semaphores. Data moves between devices by JAX's collectives and lax.ppermute only.
A program may use at most 64 MiB of HBM per device.

v0:
```python
import math

import jax
import jax.numpy as jnp
import numpy as np
from jax import lax
from jax.experimental import pallas as pl
from jax.experimental.pallas import tpu as pltpu
from jax.sharding import PartitionSpec as P

MODULUS_FLOOR = 0.5
EPSILON = 1e-05
REGULARIZER = 1.0
STEP = 64
LANES = 128
PAD = 16
BITS = 14
CHUNK = 32

F32 = jnp.float32
BF16 = jnp.bfloat16
I16 = jnp.int16


def dft_tables(points):
    index = np.arange(points)
    product = (index[:, None] * index[None, :]) % points
    angle = np.float32(2.0 * math.pi / points) * product.astype(np.float32)
    norm = 1.0 / math.sqrt(points)
    cosine = (np.cos(angle) * np.float32(norm)).astype(np.float32)
    sine = (np.sin(angle) * np.float32(norm)).astype(np.float32)
    plus = np.block([[cosine, sine], [-sine, cosine]])
    minus = np.block([[cosine, -sine], [sine, cosine]])
    return jnp.asarray(plus, BF16), jnp.asarray(minus, BF16)


def vmem_call(kernel, outs, *operands, smem=0, scratch=(), flops=0, name=None):
    specs = [pl.BlockSpec(memory_space=pltpu.SMEM)] * smem
    specs += [pl.BlockSpec(memory_space=pltpu.VMEM)] * (len(operands) - smem)
    moved = sum(math.prod(o.shape) * o.dtype.itemsize for o in (*operands, *outs))
    return pl.pallas_call(
        kernel,
        out_shape=tuple(jax.ShapeDtypeStruct(o.shape, o.dtype) for o in outs),
        in_specs=specs,
        out_specs=tuple(pl.BlockSpec(memory_space=pltpu.VMEM) for _ in outs),
        scratch_shapes=scratch,
        compiler_params=pltpu.CompilerParams(vmem_limit_bytes=40 * 1024 * 1024),
        cost_estimate=pl.CostEstimate(flops=flops, bytes_accessed=moved, transcendentals=0),
        name=name,
    )(*operands)


def shape(dims, dtype):
    return jax.ShapeDtypeStruct(dims, dtype)


def encode(block):
    peak = jnp.max(jnp.abs(block), axis=0, keepdims=True)
    power = jnp.ceil(jnp.log2(jnp.maximum(peak, 1e-30)))
    whole = jnp.round(block * jnp.exp2(BITS - power))
    return whole.astype(jnp.int32).astype(I16), power, whole * jnp.exp2(power - BITS)


def encode_to(ref, blocks):
    rows, cols = blocks[0].shape
    tail = jnp.zeros((PAD, cols), F32)
    row = lax.broadcasted_iota(jnp.int32, (PAD, cols), 0)
    decoded = []
    for n, block in enumerate(blocks):
        code, power, back = encode(block)
        ref[n * rows : (n + 1) * rows, :] = code
        tail = jnp.where(row == n, power, tail)
        decoded.append(back)
    ref[len(blocks) * rows :, :] = tail.astype(jnp.int32).astype(I16)
    return decoded


def decode(ref, count):
    rows = (ref.shape[0] - PAD) // count
    tail = ref[count * rows :, :].astype(jnp.int32).astype(F32)
    return [
        ref[n * rows : (n + 1) * rows, :].astype(jnp.int32).astype(F32) * jnp.exp2(tail[n : n + 1] - BITS)
        for n in range(count)
    ]


def turned(value):
    return pltpu.roll(value, STEP, 1)


def low_lanes(rows):
    return lax.broadcasted_iota(jnp.int32, (rows, LANES), 1) < STEP


def folded(first, second):
    mid = first.shape[0] // 2
    return jnp.concatenate([first, jnp.where(low_lanes(mid), second[:mid], turned(second[mid:]))], axis=0)


def unfolded(block):
    rows = block.shape[0] * 2 // 3
    tail, low = block[rows:], low_lanes(rows // 2)
    zero = jnp.zeros_like(tail)
    second = jnp.concatenate([jnp.where(low, tail, zero), jnp.where(low, turned(tail), zero)], axis=0)
    return jnp.concatenate([block[:rows], second], axis=1)


def frames_kernel(
    row_ref, col_ref, count_ref, own_ref, r_mine, r_other, x_mine, x_other, d_mine, d_other,
    probe_ref, amp_ref, plus_ref, minus_ref,
    lkeep_ref, lsend_ref, rkeep_ref, rsend_ref, gkeep_ref, gsend_ref, peak_ref,
    ext, patch, wave, half, field, total, grads,
):
    _, tile_rows, tile_cols = own_ref.shape
    frame = probe_ref.shape[1]
    part = r_mine.shape[1]
    mid = tile_rows // 2
    mode = lax.axis_index("mode")
    top = lax.axis_index("row") * tile_rows
    left = lax.axis_index("col") * tile_cols

    ext[:, :tile_rows, :tile_cols] = own_ref[...]
    for who, below, right, diagonal in ((mode, r_mine, x_mine, d_mine), (1 - mode, r_other, x_other, d_other)):
        rows = pl.ds(pl.multiple_of(tile_rows + who * part, 32), part)
        ext[:, rows, :tile_cols] = below[...]
        ext[:, rows, tile_cols:] = diagonal[...]
        ext[:, pl.ds(pl.multiple_of(who * mid, mid), mid), tile_cols:] = right[...]

    power = probe_ref[0] * probe_ref[0] + probe_ref[1] * probe_ref[1]
    peak_ref[...] = jnp.broadcast_to(jnp.max(power, keepdims=True), peak_ref.shape) + EPSILON

    total[...] = jnp.zeros(total.shape, F32)
    grads[...] = jnp.zeros(grads.shape, F32)
    tiles = frame // LANES
    low = low_lanes(CHUNK)

    def one(position, carry):
        row = pl.multiple_of(row_ref[position] - top, STEP)
        shift = col_ref[position] - left
        odd = (shift // STEP) % 2 == 1
        base = pl.multiple_of((shift // LANES) * LANES, LANES)

        for start in range(0, frame, CHUNK):
            rows = pl.ds(start, CHUNK)
            obj = []
            for plane in range(2):
                got = ext[plane, pl.ds(pl.multiple_of(row + start, CHUNK), CHUNK), pl.ds(base, frame + LANES)].astype(F32)
                pieces = [got[:, t * LANES : (t + 1) * LANES] for t in range(tiles + 1)]
                rolled = [turned(piece) for piece in pieces]
                chosen = [
                    jnp.where(odd, jnp.where(low, rolled[t], rolled[t + 1]), pieces[t]) for t in range(tiles)
                ]
                obj.append(jnp.concatenate(chosen, axis=1))
                patch[plane, rows, :] = obj[plane]
            p_re, p_im = probe_ref[0, rows, :], probe_ref[1, rows, :]
            wave[rows, :] = (p_re * obj[0] - p_im * obj[1]).astype(BF16)
            wave[pl.ds(frame + start, CHUNK), :] = (p_re * obj[1] + p_im * obj[0]).astype(BF16)

        def transform(left_table, right_table):
            first = jnp.dot(left_table[...], wave[...], preferred_element_type=F32)
            half[:, :frame] = first[:frame].astype(BF16)
            half[:, frame:] = first[frame:].astype(BF16)
            field[...] = jnp.dot(half[...], right_table[...], preferred_element_type=F32)

        transform(plus_ref, minus_ref)
        for start in range(0, frame, CHUNK):
            rows = pl.ds(start, CHUNK)
            re, im = field[rows, :frame], field[rows, frame:]
            inverse = jnp.minimum(lax.rsqrt(re * re + im * im), 1.0 / MODULUS_FLOOR)
            factor = amp_ref[position, rows, :].astype(F32) * inverse - 1.0
            wave[rows, :] = (re * factor).astype(BF16)
            wave[pl.ds(frame + start, CHUNK), :] = (im * factor).astype(BF16)
        transform(minus_ref, plus_ref)
        for start in range(0, frame, CHUNK):
            rows = pl.ds(start, CHUNK)
            re, im = field[rows, :frame], field[rows, frame:]
            p_re, p_im = probe_ref[0, rows, :], probe_ref[1, rows, :]
            o_re, o_im = patch[0, rows, :], patch[1, rows, :]
            steps = (p_re * re + p_im * im, p_re * im - p_im * re)
            for plane in range(2):
                pieces = [steps[plane][:, t * LANES : (t + 1) * LANES] for t in range(tiles)]
                rolled = [turned(piece) for piece in pieces]
                zero = jnp.zeros_like(pieces[0])
                moved = []
                for t in range(tiles + 1):
                    before = rolled[t - 1] if t > 0 else zero
                    here = rolled[t] if t < tiles else zero
                    moved.append(
                        jnp.where(odd, jnp.where(low, before, here), pieces[t] if t < tiles else zero)
                    )
                where = (plane, pl.ds(pl.multiple_of(row + start, CHUNK), CHUNK), pl.ds(base, frame + LANES))
                total[where] += jnp.concatenate(moved, axis=1)
            grads[0, rows, :] += o_re * re + o_im * im
            grads[1, rows, :] += o_re * im - o_im * re
            grads[2, rows, :] += o_re * o_re + o_im * o_im
        return carry

    lax.fori_loop(0, count_ref[0], one, 0)

    part_frame = frame // 2
    for who, l_ref, r_ref, g_ref in ((1 - mode, lsend_ref, rsend_ref, gsend_ref), (mode, lkeep_ref, rkeep_ref, gkeep_ref)):
        upper = pl.ds(pl.multiple_of(who * mid, mid), mid)
        lower = pl.ds(pl.multiple_of(tile_rows + who * part, 32), part)
        l_ref[:, :mid, :] = total[:, upper, :tile_cols]
        l_ref[:, mid:, :] = total[:, lower, :tile_cols]
        for plane in range(2):
            right = jnp.concatenate([total[plane, upper, tile_cols:], total[plane, lower, tile_cols:]], axis=0)
            r_ref[plane] = folded(right[:, :LANES], right[:, LANES:])
        g_ref[...] = grads[:, pl.ds(pl.multiple_of(who * part_frame, part_frame), part_frame), :]


def after_mode_kernel(rkeep, rrecv, gkeep, grecv, xsend_ref, g_ref, gsend_ref, w_ref, wsend_ref):
    encode_to(xsend_ref, [rkeep[plane] + rrecv[plane] for plane in range(2)])
    sums = [gkeep[plane] + grecv[plane] for plane in range(3)]
    g_ref[0], g_ref[1] = encode_to(gsend_ref, sums[:2])
    (w_ref[...],) = encode_to(wsend_ref, sums[2:])


def joined_kernel(g, grecv, w, wrecv, sums_ref, send_ref):
    got = decode(grecv, 2)
    sums = [g[plane] + got[plane] for plane in range(2)] + [w[...] + decode(wrecv, 1)[0]]
    sums_ref[0], sums_ref[1], sums_ref[2] = encode_to(send_ref, sums)


def split_kernel(sums, recv, g_ref, gsend_ref, w_ref, wsend_ref):
    total = [sums[plane] + got for plane, got in enumerate(decode(recv, 3))]
    g_ref[0], g_ref[1] = encode_to(gsend_ref, total[:2])
    (w_ref[...],) = encode_to(wsend_ref, total[2:])


def again_kernel(sums, recv, sums_ref, send_ref):
    total = [sums[plane] + got for plane, got in enumerate(decode(recv, 3))]
    sums_ref[0], sums_ref[1], sums_ref[2] = encode_to(send_ref, total)


def from_left_kernel(lkeep, lrecv, xrecv, tile_ref, rowsend_ref):
    rows = tile_ref.shape[1]
    came = jnp.where(lax.axis_index("col") > 0, 1.0, 0.0)
    below = []
    for plane, code in enumerate(decode(xrecv, 2)):
        got = unfolded(code) * came
        frame = got.shape[1]
        tile_ref[plane, :, :frame] = lkeep[plane, :rows, :frame] + lrecv[plane, :rows, :frame] + got[:rows]
        tile_ref[plane, :, frame:] = lkeep[plane, :rows, frame:] + lrecv[plane, :rows, frame:]
        near = lkeep[plane, rows:, :frame] + lrecv[plane, rows:, :frame] + got[rows:]
        far = lkeep[plane, rows:, frame:] + lrecv[plane, rows:, frame:]
        below.append(jnp.concatenate([near, far], axis=1))
    encode_to(rowsend_ref, below)


def from_above_kernel(rowrecv, rows_ref, spill_ref):
    got = decode(rowrecv, 2)
    came = jnp.where(lax.axis_index("row") > 0, 1.0, 0.0)
    over = spill_ref.shape[1]
    for plane in range(2):
        rows_ref[plane] = got[plane] * came
        spill_ref[plane] = got[plane][:over] * came


def object_kernel(object_ref, tile, rows, spilled, peak, out_ref):
    mode = lax.axis_index("mode")
    mid, part = tile.shape[1], rows.shape[1]
    over = mid - part
    scale = 1.0 / peak[0:1, 0:1]
    for who in range(2):

        @pl.when(mode == who)
        def _(who=who):
            for plane in range(2):
                for start in range(0, mid, CHUNK):
                    step = tile[plane, start : start + CHUNK, :]
                    if who == 0:
                        step += rows[plane, start : start + CHUNK, :] if start < part else spilled[plane, start - part :, :]
                    elif start < part - over:
                        step += rows[plane, start + over : start + over + CHUNK, :]
                    old = object_ref[who * mid + start : who * mid + start + CHUNK, plane, :]
                    out_ref[start : start + CHUNK, plane, :] = old + step * scale


def probe_kernel(g, grecv, w, wrecv, step_ref):
    weight = w[...] + decode(wrecv, 1)[0] + REGULARIZER
    got = decode(grecv, 2)
    for plane in range(2):
        step_ref[plane] = (g[plane] + got[plane]) / weight


def probe_out_kernel(probe_ref, mine, other, out_ref):
    mode = lax.axis_index("mode")
    rows = mine.shape[1]
    for start in range(0, rows, CHUNK):
        for plane in range(2):
            one, two = mine[plane, start : start + CHUNK, :], other[plane, start : start + CHUNK, :]
            first, second = jnp.where(mode == 0, one, two), jnp.where(mode == 0, two, one)
            for place, step in ((start, first), (rows + start, second)):
                old = probe_ref[place : place + CHUNK, plane, :]
                out_ref[place : place + CHUNK, plane, :] = old + step


def moved_along(value, axis, steps):
    count = lax.axis_size(axis)
    if count == 2:
        return swapped(value, axis, 1)
    first, last = (max(0, -steps), min(count, count - steps))
    return lax.ppermute(value, axis, [(source, source + steps) for source in range(first, last)])


def swapped(value, axis, distance):
    count = lax.axis_size(axis)
    return lax.ppermute(value, axis, [(source, source ^ distance) for source in range(count)])


def body(object_field, probe_field, amplitudes, row_offset, col_offset, counts):
    tile_rows, _, tile_cols = object_field.shape
    frame = probe_field.shape[0]
    halo = frame - STEP
    part, mid = halo // 2, tile_rows // 2
    rows_count, cols_count = lax.axis_size("row"), lax.axis_size("col")
    mode = lax.axis_index("mode")
    plus, minus = dft_tables(frame)

    def planar(block):
        return jnp.transpose(block.astype(BF16), (1, 0, 2))

    r_send = planar(lax.dynamic_slice_in_dim(object_field, mode * part, part, 0))
    x_send = planar(lax.dynamic_slice_in_dim(object_field[:, :, :frame], mode * mid, mid, 0))
    r_send, x_send = lax.optimization_barrier((r_send, x_send))
    d_send = r_send[:, :, :frame]
    diagonal = []
    for r in range(1, rows_count):
        for c in range(1, cols_count):
            here = r * cols_count + c
            diagonal.append((here, here - cols_count - 1))
    r_mine = moved_along(r_send, "row", -1)
    d_mine = lax.ppermute(d_send, ("row", "col"), diagonal)
    x_mine = moved_along(x_send, "col", -1)
    r_mine, d_mine, x_mine = lax.optimization_barrier((r_mine, d_mine, x_mine))
    r_other, d_other, x_other = (swapped(v, "mode", 1) for v in (r_mine, d_mine, x_mine))
    own = planar(object_field)
    probe = jnp.transpose(probe_field, (1, 0, 2))

    held = mid + part
    l_shape = shape((2, held, tile_cols), F32)
    r_shape = shape((2, held * 3 // 2, LANES), F32)
    g_shape = shape((3, frame // 2, frame), F32)
    lkeep, lsend, rkeep, rsend, gkeep, gsend, peak = vmem_call(
        frames_kernel,
        (l_shape, l_shape, r_shape, r_shape, g_shape, g_shape, shape((8, LANES), F32)),
        row_offset, col_offset, counts, own, r_mine, r_other, x_mine, x_other, d_mine, d_other,
        probe, amplitudes, plus, minus,
        smem=3,
        scratch=[
            pltpu.VMEM((2, tile_rows + halo, tile_cols + frame), BF16),
            pltpu.VMEM((2, frame, frame), F32),
            pltpu.VMEM((2 * frame, frame), BF16),
            pltpu.VMEM((frame, 2 * frame), BF16),
            pltpu.VMEM((frame, 2 * frame), F32),
            pltpu.VMEM((2, tile_rows + halo, tile_cols + frame), F32),
            pltpu.VMEM((3, frame, frame), F32),
        ],
        flops=4 * 32 * frame**3,
        name="frames",
    )
    rrecv = swapped(rsend, "mode", 1)
    grecv = swapped(gsend, "mode", 1)
    rrecv, grecv, lsend = lax.optimization_barrier((rrecv, grecv, lsend))
    lrecv = swapped(lsend, "mode", 1)

    quarter = frame // 2
    g_out = (shape((2, quarter, frame), F32), shape((2 * quarter + PAD, frame), I16))
    w_out = (shape((quarter, frame), F32), shape((quarter + PAD, frame), I16))
    all_out = (shape((3, quarter, frame), F32), shape((3 * quarter + PAD, frame), I16))
    row_steps = [("row", 1 << k) for k in range(rows_count.bit_length() - 1)]
    col_steps = [("col", 1 << k) for k in range(cols_count.bit_length() - 1)]

    xsend, g, gcode, w, wcode = vmem_call(
        after_mode_kernel, (shape((held * 3 + PAD, LANES), I16), *g_out, *w_out),
        rkeep, rrecv, gkeep, grecv, name="after_mode",
    )
    xrecv = moved_along(xsend, "col", 1)
    gother, wother = swapped(gcode, *row_steps[0]), swapped(wcode, *row_steps[1])
    sums, code = vmem_call(joined_kernel, all_out, g, gother, w, wother, name="joined")
    xrecv, code = lax.optimization_barrier((xrecv, code))
    came = swapped(code, *col_steps[0])
    tile, rowsend = vmem_call(
        from_left_kernel,
        (shape((2, mid, tile_cols), F32), shape((2 * part + PAD, tile_cols), I16)),
        lkeep, lrecv, xrecv, name="from_left",
    )
    rowrecv = moved_along(rowsend, "row", 1)
    for step in row_steps[2:] + col_steps[1:]:
        sums, code = vmem_call(again_kernel, all_out, sums, came, name="again")
        came = swapped(code, *step)
    g, gcode, w, wcode = vmem_call(split_kernel, (*g_out, *w_out), sums, came, name="split")
    gother, wother = swapped(gcode, *row_steps[1]), swapped(wcode, *row_steps[0])

    rowrecv, w = lax.optimization_barrier((rowrecv, w))
    rows, spill = vmem_call(
        from_above_kernel,
        (shape((2, part, tile_cols), F32), shape((2, mid - part, tile_cols), F32)), rowrecv, name="from_above",
    )
    spilled = swapped(spill, "mode", 1)
    (object_new,) = vmem_call(
        object_kernel, (shape((mid, 2, tile_cols), F32),), object_field, tile, rows, spilled, peak, name="object"
    )
    object_new, gother = lax.optimization_barrier((object_new, gother))
    (step,) = vmem_call(probe_kernel, (shape((2, quarter, frame), F32),), g, gother, w, wother, name="probe")
    other = swapped(step, "mode", 1)
    (probe_new,) = vmem_call(
        probe_out_kernel, (shape(probe_field.shape, F32),), probe_field, step, other, name="probe_out"
    )
    return (object_new, probe_new)


def solution(mesh):
    placed = (
        P(("groups", "row"), None, "col"),
        P("groups", None, None),
        P(("groups", "row", "col", "mode"), None, None),
        P(("groups", "row", "col", "mode")),
        P(("groups", "row", "col", "mode")),
        P(("groups", "row", "col", "mode")),
    )
    return jax.shard_map(
        body,
        mesh=mesh,
        in_specs=placed,
        out_specs=(P(("groups", "row", "mode"), None, "col"), P("groups", None, None)),
        check_vma=False,
    )
```

profile of v0, /device:TPU:0, one launch (start us, length us, event | category | flops | bytes accessed | tf_op | source)
XLA Modules:
  0.0 59.2 jit_solution(18089068755340845980)
XLA Ops:
  0.6 1.4 %copy.18 = bf16[256,2,512]{2,0,1:T(8,128)(2,1)S(1)} copy(f32[256,2,512]{2,1,0:T(2,128)} %object_ref.1) | data formatting | bytes 1572864 | tf_op args[0]
  2.0 0.0 copy-start.6
  2.1 0.0 copy-start.1
  2.1 1.4 %collective-permute-start = (bf16[2,96,512]{2,1,0:T(8,128)(2,1)S(1)}, bf16[2,96,512]{2,1,0:T(8,128)(2,1)S(1)}, u32[]{:S(2)}, u32[]{:S(2)}) collective-permute-start(bf16[2,96,512]{2,1,0:T(8,128)(2,1)S(1)} %fusion), channel_id=1, source_target_pairs={{4,0},{8,4},{12,8},{5,1},{9,5},{13,9},{6,2},{10,6},{14,10},{7,3},{... | collective-permute-start | bytes 589832 | tf_op jit(solution)/shard_map/ppermute | solution.py:304
  3.6 3.0 %collective-permute-start.2 = (bf16[2,128,256]{2,1,0:T(8,128)(2,1)S(1)}, bf16[2,128,256]{2,1,0:T(8,128)(2,1)S(1)}, u32[]{:S(2)}, u32[]{:S(2)}) collective-permute-start(bf16[2,128,256]{2,1,0:T(8,128)(2,1)S(1)} %fusion.1), channel_id=1, source_target_pairs={{0,2},{2,0},{1,3},{3,1},{4,6},{6,4},{5,7},{7,5},{8,10},{10,8},{9,1... | collective-permute-start | bytes 393224 | tf_op jit(solution)/shard_map/ppermute | solution.py:309
  6.6 1.3 %collective-permute-start.1 = (bf16[2,96,256]{2,1,0:T(8,128)(2,1)S(1)}, bf16[2,96,256]{2,1,0:T(8,128)(2,1)S(1)}, u32[]{:S(2)}, u32[]{:S(2)}) collective-permute-start(bf16[2,96,256]{2,1,0:T(8,128)(2,1)S(1)} %slice.7), channel_id=1, source_target_pairs={{6,0},{10,4},{14,8},{7,1},{11,5},{15,9},{22,16},{26,20},{30,24},{2... | collective-permute-start | bytes 294920 | tf_op jit(solution)/shard_map/ppermute | solution.py:334
  7.9 7.4 %collective-permute-done.1.d_mine = bf16[2,96,256]{2,1,0:T(8,128)(2,1)S(1)} collective-permute-done((bf16[2,96,256]{2,1,0:T(8,128)(2,1)S(1)}, bf16[2,96,256]{2,1,0:T(8,128)(2,1)S(1)}, u32[]{:S(2)}, u32[]{:S(2)}) %collective-permute-start.1) | collective-permute-done | bytes 98336 | tf_op jit(solution)/shard_map/ppermute | solution.py:334
  15.3 0.0 collective-permute-done.2.x_mine
  15.3 0.0 collective-permute-done.r_mine
  15.3 0.0 collective-permute-start.3
  15.3 0.5 collective-permute-start.4
  15.8 0.1 collective-permute-start.5
  16.5 0.0 copy-done.1
  16.5 0.0 copy-start.2
  16.5 0.0 copy-start.5
  16.6 0.5 collective-permute-done.5.d_other
  17.1 0.0 collective-permute-done.4.x_other
  17.1 0.0 collective-permute-done.3.r_other
  17.1 0.0 copy-start.3
  17.1 0.0 copy-start.4
  17.1 0.0 copy-done.6
  17.1 0.4 copy-done.2
  17.6 0.2 copy-done.5
  17.7 0.1 copy-done.3
  17.8 0.0 copy-done.4
  17.9 8.4 %frames.1 = (f32[2,224,512]{2,1,0:T(8,128)S(1)}, f32[2,224,512]{2,1,0:T(8,128)S(1)}, f32[2,336,128]{2,1,0:T(8,128)S(1)}, f32[2,336,128]{2,1,0:T(8,128)S(1)}, f32...) custom-call(s32[4]{0:T(128)S(1)} %copy-done.3, s32[4]{0:T(128)S(1)} %copy-done.4, ...), custom_call_target="tpu_custom_call" | custom-call | flops 2147483648 | bytes 6787108 | tf_op jit(solution)/shard_map/frames/pallas_call | solution.py:41
  26.3 0.1 collective-permute-start.7
  26.4 0.5 collective-permute-start.6
  26.9 1.7 %collective-permute-done.6.rrecv = f32[2,336,128]{2,1,0:T(8,128)S(1)} collective-permute-done((f32[2,336,128]{2,1,0:T(8,128)S(1)}, f32[2,336,128]{2,1,0:T(8,128)S(1)}, u32[]{:S(2)}, u32[]{:S(2)}) %collective-permute-start.6) | collective-permute-done | bytes 344096 | tf_op jit(solution)/shard_map/ppermute | solution.py:309
  28.6 0.0 collective-permute-done.7.grecv
  28.6 0.1 collective-permute-start.8
  28.7 0.2 after_mode.1
  28.9 0.1 collective-permute-start.9
  29.0 0.1 collective-permute-start.10
  29.1 2.7 %collective-permute-start.11 = (s16[144,256]{1,0:T(8,128)(2,1)S(1)}, s16[144,256]{1,0:T(8,128)(2,1)S(1)}, u32[]{:S(2)}, u32[]{:S(2)}) collective-permute-start(s16[144,256]{1,0:T(8,128)(2,1)S(1)} %get-tuple-element.56), channel_id=1, source_target_pairs={{0,8},{4,12},{8,0},{12,4},{1,9},{5,13},{9,1},{13,5},{2,10},{6,14},... | collective-permute-start | bytes 221192 | tf_op jit(solution)/shard_map/ppermute | solution.py:309
  31.8 2.9 %collective-permute-done.11.wrecv = s16[144,256]{1,0:T(8,128)(2,1)S(1)} collective-permute-done((s16[144,256]{1,0:T(8,128)(2,1)S(1)}, s16[144,256]{1,0:T(8,128)(2,1)S(1)}, u32[]{:S(2)}, u32[]{:S(2)}) %collective-permute-start.11) | collective-permute-done | bytes 73760 | tf_op jit(solution)/shard_map/ppermute | solution.py:309
  34.7 1.9 %collective-permute-done.10.grecv = s16[272,256]{1,0:T(8,128)(2,1)S(1)} collective-permute-done((s16[272,256]{1,0:T(8,128)(2,1)S(1)}, s16[272,256]{1,0:T(8,128)(2,1)S(1)}, u32[]{:S(2)}, u32[]{:S(2)}) %collective-permute-start.10) | collective-permute-done | bytes 139296 | tf_op jit(solution)/shard_map/ppermute | solution.py:309
  36.6 0.1 joined.1
  36.8 0.0 collective-permute-done.9.xrecv
  36.8 0.0 collective-permute-done.8.lrecv
  36.8 0.0 copy-start
  36.8 0.2 from_left.1
  37.0 4.6 %collective-permute-start.12 = (s16[208,512]{1,0:T(8,128)(2,1)S(1)}, s16[208,512]{1,0:T(8,128)(2,1)S(1)}, u32[]{:S(2)}, u32[]{:S(2)}) collective-permute-start(s16[208,512]{1,0:T(8,128)(2,1)S(1)} %get-tuple-element.60), channel_id=1, source_target_pairs={{0,4},{4,8},{8,12},{1,5},{5,9},{9,13},{2,6},{6,10},{10,14},{3,7},{... | collective-permute-start | bytes 638984 | tf_op jit(solution)/shard_map/ppermute | solution.py:304
  41.7 1.7 %collective-permute-start.13 = (s16[400,256]{1,0:T(8,128)(2,1)S(1)}, s16[400,256]{1,0:T(8,128)(2,1)S(1)}, u32[]{:S(2)}, u32[]{:S(2)}) collective-permute-start(s16[400,256]{1,0:T(8,128)(2,1)S(1)} %get-tuple-element.62), channel_id=1, source_target_pairs={{0,2},{2,0},{1,3},{3,1},{4,6},{6,4},{5,7},{7,5},{8,10},{10,8},{9,1... | collective-permute-start | bytes 614408 | tf_op jit(solution)/shard_map/ppermute | solution.py:309
  43.4 4.6 %collective-permute-done.13.recv = s16[400,256]{1,0:T(8,128)(2,1)S(1)} collective-permute-done((s16[400,256]{1,0:T(8,128)(2,1)S(1)}, s16[400,256]{1,0:T(8,128)(2,1)S(1)}, u32[]{:S(2)}, u32[]{:S(2)}) %collective-permute-start.13) | collective-permute-done | bytes 204832 | tf_op jit(solution)/shard_map/ppermute | solution.py:309
  48.0 0.1 split.1
  48.2 1.4 %collective-permute-start.15 = (s16[272,256]{1,0:T(8,128)(2,1)S(1)}, s16[272,256]{1,0:T(8,128)(2,1)S(1)}, u32[]{:S(2)}, u32[]{:S(2)}) collective-permute-start(s16[272,256]{1,0:T(8,128)(2,1)S(1)} %get-tuple-element.68), channel_id=1, source_target_pairs={{0,8},{4,12},{8,0},{12,4},{1,9},{5,13},{9,1},{13,5},{2,10},{6,14},... | collective-permute-start | bytes 417800 | tf_op jit(solution)/shard_map/ppermute | solution.py:309
  49.5 0.0 collective-permute-done.12.rowrecv
  49.5 0.1 from_above.1
  49.6 0.1 collective-permute-start.14
  49.7 0.1 collective-permute-start.16
  49.8 1.3 %collective-permute-done.14.spilled = f32[2,32,512]{2,1,0:T(8,128)S(1)} collective-permute-done((f32[2,32,512]{2,1,0:T(8,128)S(1)}, f32[2,32,512]{2,1,0:T(8,128)S(1)}, u32[]{:S(2)}, u32[]{:S(2)}) %collective-permute-start.14) | collective-permute-done | bytes 131104 | tf_op jit(solution)/shard_map/ppermute | solution.py:309
  51.0 0.0 copy-done
  51.0 1.1 %object.1 = f32[128,2,512]{2,1,0:T(2,128)} custom-call(f32[256,2,512]{2,1,0:T(2,128)S(1)} %copy-done, f32[2,128,512]{2,1,0:T(8,128)S(1)} %get-tuple-element.59.tile, f32[2,96,512]{2,1,0:T(8,128)S(1)} %get-tuple-element.65.rows, f32[2,32,512]{2,1,0:T(8,128)S(1)} %collective-permute-done.14.spilled, f32[8,128]{1,0:T(8,128)S(1)} %get-tuple-element.67.peak), custom_call_target="tpu_custom_call" | custom-call | bytes 2625536 | tf_op jit(solution)/shard_map/object/pallas_call | solution.py:41
  52.1 4.1 %collective-permute-done.15.grecv = s16[272,256]{1,0:T(8,128)(2,1)S(1)} collective-permute-done((s16[272,256]{1,0:T(8,128)(2,1)S(1)}, s16[272,256]{1,0:T(8,128)(2,1)S(1)}, u32[]{:S(2)}, u32[]{:S(2)}) %collective-permute-start.15) | collective-permute-done | bytes 139296 | tf_op jit(solution)/shard_map/ppermute | solution.py:309
  56.1 0.3 collective-permute-done.16.wrecv
  56.4 0.1 probe.1.mine
  56.5 0.1 collective-permute-start.17
  56.6 1.5 %collective-permute-done.17.other = f32[2,128,256]{2,1,0:T(8,128)S(1)} collective-permute-done((f32[2,128,256]{2,1,0:T(8,128)S(1)}, f32[2,128,256]{2,1,0:T(8,128)S(1)}, u32[]{:S(2)}, u32[]{:S(2)}) %collective-permute-start.17) | collective-permute-done | bytes 262176 | tf_op jit(solution)/shard_map/ppermute | solution.py:309
  58.1 1.1 %probe_out.1 = f32[256,2,256]{2,1,0:T(2,128)} custom-call(f32[256,2,256]{2,1,0:T(2,128)S(1)} %copy-done.1, f32[2,128,256]{2,1,0:T(8,128)S(1)} %probe.1.mine, f32[2,128,256]{2,1,0:T(8,128)S(1)} %collective-permute-done.17.other), custom_call_target="tpu_custom_call" | custom-call | bytes 1572864 | tf_op jit(solution)/shard_map/probe_out/pallas_call | solution.py:41
  (5 shorter events, 0.1 us)
Async XLA Ops:
  2.0 15.1 %copy-start.6 = (bf16[512,512]{1,0:T(8,128)(2,1)S(1)}, bf16[512,512]{1,0:T(8,128)(2,1)}, u32[]{:S(2)}) copy-start(bf16[512,512]{1,0:T(8,128)(2,1)} %constant.16.clone.plus_ref) | copy-start | bytes 1572868
  2.1 14.5 %copy-start.1 = (f32[256,2,256]{2,1,0:T(2,128)S(1)}, f32[256,2,256]{2,1,0:T(2,128)}, u32[]{:S(2)}) copy-start(f32[256,2,256]{2,1,0:T(2,128)} %probe_ref.1) | copy-start | bytes 1572868
  2.1 13.2 %collective-permute-start = (bf16[2,96,512]{2,1,0:T(8,128)(2,1)S(1)}, bf16[2,96,512]{2,1,0:T(8,128)(2,1)S(1)}, u32[]{:S(2)}, u32[]{:S(2)}) collective-permute-start(bf16[2,96,512]{2,1,0:T(8,128)(2,1)S(1)} %fusion), channel_id=1, source_target_pairs={{4,0},{8,4},{12,8},{5,1},{9,5},{13,9},{6,2},{10,6},{14,10},{7,3},{... | collective-permute-start | bytes 589832 | tf_op jit(solution)/shard_map/ppermute | solution.py:304
  3.6 11.7 %collective-permute-start.2 = (bf16[2,128,256]{2,1,0:T(8,128)(2,1)S(1)}, bf16[2,128,256]{2,1,0:T(8,128)(2,1)S(1)}, u32[]{:S(2)}, u32[]{:S(2)}) collective-permute-start(bf16[2,128,256]{2,1,0:T(8,128)(2,1)S(1)} %fusion.1), channel_id=1, source_target_pairs={{0,2},{2,0},{1,3},{3,1},{4,6},{6,4},{5,7},{7,5},{8,10},{10,8},{9,1... | collective-permute-start | bytes 393224 | tf_op jit(solution)/shard_map/ppermute | solution.py:309
  6.6 8.7 %collective-permute-start.1 = (bf16[2,96,256]{2,1,0:T(8,128)(2,1)S(1)}, bf16[2,96,256]{2,1,0:T(8,128)(2,1)S(1)}, u32[]{:S(2)}, u32[]{:S(2)}) collective-permute-start(bf16[2,96,256]{2,1,0:T(8,128)(2,1)S(1)} %slice.7), channel_id=1, source_target_pairs={{6,0},{10,4},{14,8},{7,1},{11,5},{15,9},{22,16},{26,20},{30,24},{2... | collective-permute-start | bytes 294920 | tf_op jit(solution)/shard_map/ppermute | solution.py:334
  15.3 1.8 %collective-permute-start.3 = (bf16[2,96,512]{2,1,0:T(8,128)(2,1)S(1)}, bf16[2,96,512]{2,1,0:T(8,128)(2,1)S(1)}, u32[]{:S(2)}, u32[]{:S(2)}) collective-permute-start(bf16[2,96,512]{2,1,0:T(8,128)(2,1)S(1)} %collective-permute-done.r_mine), channel_id=1, source_target_pairs={{0,1},{1,0},{2,3},{3,2},{4,5},{5,4},{6,7},{7,6},{8,9},{9,8},{10,11... | collective-permute-start | bytes 589832 | tf_op jit(solution)/shard_map/ppermute | solution.py:309
  15.3 1.8 %collective-permute-start.4 = (bf16[2,128,256]{2,1,0:T(8,128)(2,1)S(1)}, bf16[2,128,256]{2,1,0:T(8,128)(2,1)S(1)}, u32[]{:S(2)}, u32[]{:S(2)}) collective-permute-start(bf16[2,128,256]{2,1,0:T(8,128)(2,1)S(1)} %collective-permute-done.2.x_mine), channel_id=1, source_target_pairs={{0,1},{1,0},{2,3},{3,2},{4,5},{5,4},{6,7},{7,6},{8,9},{9,8},{10,11... | collective-permute-start | bytes 393224 | tf_op jit(solution)/shard_map/ppermute | solution.py:309
  15.8 1.3 %collective-permute-start.5 = (bf16[2,96,256]{2,1,0:T(8,128)(2,1)S(1)}, bf16[2,96,256]{2,1,0:T(8,128)(2,1)S(1)}, u32[]{:S(2)}, u32[]{:S(2)}) collective-permute-start(bf16[2,96,256]{2,1,0:T(8,128)(2,1)S(1)} %collective-permute-done.1.d_mine), channel_id=1, source_target_pairs={{0,1},{1,0},{2,3},{3,2},{4,5},{5,4},{6,7},{7,6},{8,9},{9,8},{10,11... | collective-permute-start | bytes 294920 | tf_op jit(solution)/shard_map/ppermute | solution.py:309
  16.5 1.0 %copy-start.2 = (bf16[4,256,256]{2,1,0:T(8,128)(2,1)S(1)}, bf16[4,256,256]{2,1,0:T(8,128)(2,1)}, u32[]{:S(2)}) copy-start(bf16[4,256,256]{2,1,0:T(8,128)(2,1)} %amp_ref.1) | copy-start | bytes 1572868
  16.5 1.2 %copy-start.5 = (bf16[512,512]{1,0:T(8,128)(2,1)S(1)}, bf16[512,512]{1,0:T(8,128)(2,1)}, u32[]{:S(2)}) copy-start(bf16[512,512]{1,0:T(8,128)(2,1)} %constant.17.clone.minus_ref) | copy-start | bytes 1572868
  17.1 0.7 %copy-start.3 = (s32[4]{0:T(128)S(1)}, s32[4]{0:T(128)}, u32[]{:S(2)}) copy-start(s32[4]{0:T(128)} %row_ref.1) | copy-start | bytes 52
  17.1 0.7 %copy-start.4 = (s32[4]{0:T(128)S(1)}, s32[4]{0:T(128)}, u32[]{:S(2)}) copy-start(s32[4]{0:T(128)} %col_ref.1) | copy-start | bytes 52
  26.3 2.3 %collective-permute-start.7 = (f32[3,128,256]{2,1,0:T(8,128)S(1)}, f32[3,128,256]{2,1,0:T(8,128)S(1)}, u32[]{:S(2)}, u32[]{:S(2)}) collective-permute-start(f32[3,128,256]{2,1,0:T(8,128)S(1)} %get-tuple-element.45), channel_id=1, source_target_pairs={{0,1},{1,0},{2,3},{3,2},{4,5},{5,4},{6,7},{7,6},{8,9},{9,8},{10,11... | collective-permute-start | bytes 1179656 | tf_op jit(solution)/shard_map/ppermute | solution.py:309
  26.4 2.2 %collective-permute-start.6 = (f32[2,336,128]{2,1,0:T(8,128)S(1)}, f32[2,336,128]{2,1,0:T(8,128)S(1)}, u32[]{:S(2)}, u32[]{:S(2)}) collective-permute-start(f32[2,336,128]{2,1,0:T(8,128)S(1)} %get-tuple-element.44), channel_id=1, source_target_pairs={{0,1},{1,0},{2,3},{3,2},{4,5},{5,4},{6,7},{7,6},{8,9},{9,8},{10,11... | collective-permute-start | bytes 1032200 | tf_op jit(solution)/shard_map/ppermute | solution.py:309
  28.6 8.2 %collective-permute-start.8 = (f32[2,224,512]{2,1,0:T(8,128)S(1)}, f32[2,224,512]{2,1,0:T(8,128)S(1)}, u32[]{:S(2)}, u32[]{:S(2)}) collective-permute-start(f32[2,224,512]{2,1,0:T(8,128)S(1)} %get-tuple-element.47), channel_id=1, source_target_pairs={{0,1},{1,0},{2,3},{3,2},{4,5},{5,4},{6,7},{7,6},{8,9},{9,8},{10,11... | collective-permute-start | bytes 2752520 | tf_op jit(solution)/shard_map/ppermute | solution.py:309
  28.9 7.8 %collective-permute-start.9 = (s16[688,128]{1,0:T(8,128)(2,1)S(1)}, s16[688,128]{1,0:T(8,128)(2,1)S(1)}, u32[]{:S(2)}, u32[]{:S(2)}) collective-permute-start(s16[688,128]{1,0:T(8,128)(2,1)S(1)} %get-tuple-element.52), channel_id=1, source_target_pairs={{0,2},{2,0},{1,3},{3,1},{4,6},{6,4},{5,7},{7,5},{8,10},{10,8},{9,1... | collective-permute-start | bytes 528392 | tf_op jit(solution)/shard_map/ppermute | solution.py:309
  29.0 7.6 %collective-permute-start.10 = (s16[272,256]{1,0:T(8,128)(2,1)S(1)}, s16[272,256]{1,0:T(8,128)(2,1)S(1)}, u32[]{:S(2)}, u32[]{:S(2)}) collective-permute-start(s16[272,256]{1,0:T(8,128)(2,1)S(1)} %get-tuple-element.54), channel_id=1, source_target_pairs={{0,4},{4,0},{8,12},{12,8},{1,5},{5,1},{9,13},{13,9},{2,6},{6,2},{1... | collective-permute-start | bytes 417800 | tf_op jit(solution)/shard_map/ppermute | solution.py:309
  29.1 5.6 %collective-permute-start.11 = (s16[144,256]{1,0:T(8,128)(2,1)S(1)}, s16[144,256]{1,0:T(8,128)(2,1)S(1)}, u32[]{:S(2)}, u32[]{:S(2)}) collective-permute-start(s16[144,256]{1,0:T(8,128)(2,1)S(1)} %get-tuple-element.56), channel_id=1, source_target_pairs={{0,8},{4,12},{8,0},{12,4},{1,9},{5,13},{9,1},{13,5},{2,10},{6,14},... | collective-permute-start | bytes 221192 | tf_op jit(solution)/shard_map/ppermute | solution.py:309
  36.8 14.2 %copy-start = (f32[256,2,512]{2,1,0:T(2,128)S(1)}, f32[256,2,512]{2,1,0:T(2,128)}, u32[]{:S(2)}) copy-start(f32[256,2,512]{2,1,0:T(2,128)} %object_ref.1) | copy-start | bytes 3145732
  37.0 12.5 %collective-permute-start.12 = (s16[208,512]{1,0:T(8,128)(2,1)S(1)}, s16[208,512]{1,0:T(8,128)(2,1)S(1)}, u32[]{:S(2)}, u32[]{:S(2)}) collective-permute-start(s16[208,512]{1,0:T(8,128)(2,1)S(1)} %get-tuple-element.60), channel_id=1, source_target_pairs={{0,4},{4,8},{8,12},{1,5},{5,9},{9,13},{2,6},{6,10},{10,14},{3,7},{... | collective-permute-start | bytes 638984 | tf_op jit(solution)/shard_map/ppermute | solution.py:304
  41.7 6.3 %collective-permute-start.13 = (s16[400,256]{1,0:T(8,128)(2,1)S(1)}, s16[400,256]{1,0:T(8,128)(2,1)S(1)}, u32[]{:S(2)}, u32[]{:S(2)}) collective-permute-start(s16[400,256]{1,0:T(8,128)(2,1)S(1)} %get-tuple-element.62), channel_id=1, source_target_pairs={{0,2},{2,0},{1,3},{3,1},{4,6},{6,4},{5,7},{7,5},{8,10},{10,8},{9,1... | collective-permute-start | bytes 614408 | tf_op jit(solution)/shard_map/ppermute | solution.py:309
  48.2 8.0 %collective-permute-start.15 = (s16[272,256]{1,0:T(8,128)(2,1)S(1)}, s16[272,256]{1,0:T(8,128)(2,1)S(1)}, u32[]{:S(2)}, u32[]{:S(2)}) collective-permute-start(s16[272,256]{1,0:T(8,128)(2,1)S(1)} %get-tuple-element.68), channel_id=1, source_target_pairs={{0,8},{4,12},{8,0},{12,4},{1,9},{5,13},{9,1},{13,5},{2,10},{6,14},... | collective-permute-start | bytes 417800 | tf_op jit(solution)/shard_map/ppermute | solution.py:309
  49.6 1.4 %collective-permute-start.14 = (f32[2,32,512]{2,1,0:T(8,128)S(1)}, f32[2,32,512]{2,1,0:T(8,128)S(1)}, u32[]{:S(2)}, u32[]{:S(2)}) collective-permute-start(f32[2,32,512]{2,1,0:T(8,128)S(1)} %get-tuple-element.66), channel_id=1, source_target_pairs={{0,1},{1,0},{2,3},{3,2},{4,5},{5,4},{6,7},{7,6},{8,9},{9,8},{10,11... | collective-permute-start | bytes 393224 | tf_op jit(solution)/shard_map/ppermute | solution.py:309
  49.7 6.7 %collective-permute-start.16 = (s16[144,256]{1,0:T(8,128)(2,1)S(1)}, s16[144,256]{1,0:T(8,128)(2,1)S(1)}, u32[]{:S(2)}, u32[]{:S(2)}) collective-permute-start(s16[144,256]{1,0:T(8,128)(2,1)S(1)} %get-tuple-element.73), channel_id=1, source_target_pairs={{0,4},{4,0},{8,12},{12,8},{1,5},{5,1},{9,13},{13,9},{2,6},{6,2},{1... | collective-permute-start | bytes 221192 | tf_op jit(solution)/shard_map/ppermute | solution.py:309
  56.5 1.6 %collective-permute-start.17 = (f32[2,128,256]{2,1,0:T(8,128)S(1)}, f32[2,128,256]{2,1,0:T(8,128)S(1)}, u32[]{:S(2)}, u32[]{:S(2)}) collective-permute-start(f32[2,128,256]{2,1,0:T(8,128)S(1)} %probe.1.mine), channel_id=1, source_target_pairs={{0,1},{1,0},{2,3},{3,2},{4,5},{5,4},{6,7},{7,6},{8,9},{9,8},{10,11... | collective-permute-start | bytes 786440 | tf_op jit(solution)/shard_map/ppermute | solution.py:309
where the time goes:
time: 58.6 us; the launch traced here: 59.2 us
  waiting for transfers between devices  26.2 us (45%)
  starting transfers between devices  17.8 us (30%)
  Pallas kernels  11.5 us (20%)
  local copies, waits for them, and re-layouts  2.25 us (4%)
  between operations  1.53 us (3%)
    ppermute x15, waiting for transfers between devices, swapped(): lax.ppermute(value, axis, [(source, source ^ distance) for source in rang...  18.7 us
    pallas_call x9, Pallas kernels, vmem_call(): pl.pallas_call(kernel, out_shape=tuple((jax.ShapeDtypeStruct(o.shape, o.d...  11.5 us
    ppermute x15, starting transfers between devices, swapped(): lax.ppermute(value, axis, [(source, source ^ distance) for source in rang...  10.4 us
    ppermute x1, waiting for transfers between devices, body(): d_mine = lax.ppermute(d_send, ('row', 'col'), diagonal)  7.41 us
    ppermute x2, starting transfers between devices, moved_along(): lax.ppermute(value, axis, [(source, source + steps) for source in range(f...  6.07 us
    unnamed x16, local copies, waits for them, and re-layouts  2.18 us
    ppermute x1, starting transfers between devices, body(): d_mine = lax.ppermute(d_send, ('row', 'col'), diagonal)  1.29 us
  transfers between devices with their start and end apart: 18, of which 10 were waited for; matrix products, arithmetic and copies ran while one was open for 0% of the time, Pallas kernels for 3%

commit v1 on v0

--- a/solution.py
+++ b/solution.py
@@ -16,6 +16,8 @@
 PAD = 16
 BITS = 14
 CHUNK = 32
+GROUP = 2
+STAGGER = 2
 
 F32 = jnp.float32
 BF16 = jnp.bfloat16
@@ -134,51 +136,63 @@
     tiles = frame // LANES
     low = low_lanes(CHUNK)
 
-    def one(position, carry):
-        row = pl.multiple_of(row_ref[position] - top, STEP)
-        shift = col_ref[position] - left
-        odd = (shift // STEP) % 2 == 1
-        base = pl.multiple_of((shift // LANES) * LANES, LANES)
-
+    count = amp_ref.shape[0]
+    base_row = [pl.multiple_of(row_ref[n] - top, STEP) for n in range(count)]
+    shift = [col_ref[n] - left for n in range(count)]
+    odd = [(shift[n] // STEP) % 2 == 1 for n in range(count)]
+    base_col = [pl.multiple_of((shift[n] // LANES) * LANES, LANES) for n in range(count)]
+    live = [jnp.where(n < count_ref[0], 1.0, 0.0) for n in range(count)]
+
+    def window(n, plane, start):
+        rows = pl.ds(pl.multiple_of(base_row[n] + start, CHUNK), CHUNK)
+        return plane, rows, pl.ds(base_col[n], frame + LANES)
+
+    def tile_of(value, t):
+        return value[:, t * LANES : (t + 1) * LANES]
+
+    def exit_wave(n):
         for start in range(0, frame, CHUNK):
             rows = pl.ds(start, CHUNK)
             obj = []
             for plane in range(2):
-                got = ext[plane, pl.ds(pl.multiple_of(row + start, CHUNK), CHUNK), pl.ds(base, frame + LANES)].astype(F32)
-                pieces = [got[:, t * LANES : (t + 1) * LANES] for t in range(tiles + 1)]
+                got = ext[window(n, plane, start)].astype(F32)
+                pieces = [tile_of(got, t) for t in range(tiles + 1)]
                 rolled = [turned(piece) for piece in pieces]
                 chosen = [
-                    jnp.where(odd, jnp.where(low, rolled[t], rolled[t + 1]), pieces[t]) for t in range(tiles)
+                    jnp.where(odd[n], jnp.where(low, rolled[t], rolled[t + 1]), pieces[t]) for t in range(tiles)
                 ]
                 obj.append(jnp.concatenate(chosen, axis=1))
-                patch[plane, rows, :] = obj[plane]
+                patch[n, plane, rows, :] = obj[plane].astype(BF16)
             p_re, p_im = probe_ref[0, rows, :], probe_ref[1, rows, :]
-            wave[rows, :] = (p_re * obj[0] - p_im * obj[1]).astype(BF16)
-            wave[pl.ds(frame + start, CHUNK), :] = (p_re * obj[1] + p_im * obj[0]).astype(BF16)
-
-        def transform(left_table, right_table):
-            first = jnp.dot(left_table[...], wave[...], preferred_element_type=F32)
-            half[:, :frame] = first[:frame].astype(BF16)
-            half[:, frame:] = first[frame:].astype(BF16)
-            field[...] = jnp.dot(half[...], right_table[...], preferred_element_type=F32)
-
-        transform(plus_ref, minus_ref)
+            wave[n, rows, :] = (p_re * obj[0] - p_im * obj[1]).astype(BF16)
+            wave[n, pl.ds(frame + start, CHUNK), :] = (p_re * obj[1] + p_im * obj[0]).astype(BF16)
+
+    def left_product(n, table):
+        first = jnp.dot(table[...], wave[n], preferred_element_type=F32)
+        half[n, :, :frame] = first[:frame].astype(BF16)
+        half[n, :, frame:] = first[frame:].astype(BF16)
+
+    def right_product(n, table):
+        field[n] = jnp.dot(half[n], table[...], preferred_element_type=F32)
+
+    def change(n):
         for start in range(0, frame, CHUNK):
             rows = pl.ds(start, CHUNK)
-            re, im = field[rows, :frame], field[rows, frame:]
+            re, im = field[n, rows, :frame], field[n, rows, frame:]
             inverse = jnp.minimum(lax.rsqrt(re * re + im * im), 1.0 / MODULUS_FLOOR)
-            factor = amp_ref[position, rows, :].astype(F32) * inverse - 1.0
-            wave[rows, :] = (re * factor).astype(BF16)
-            wave[pl.ds(frame + start, CHUNK), :] = (im * factor).astype(BF16)
-        transform(minus_ref, plus_ref)
+            factor = (amp_ref[n, rows, :].astype(F32) * inverse - 1.0) * live[n]
+            wave[n, rows, :] = (re * factor).astype(BF16)
+            wave[n, pl.ds(frame + start, CHUNK), :] = (im * factor).astype(BF16)
+
+    def update(n):
         for start in range(0, frame, CHUNK):
             rows = pl.ds(start, CHUNK)
-            re, im = field[rows, :frame], field[rows, frame:]
+            re, im = field[n, rows, :frame], field[n, rows, frame:]
             p_re, p_im = probe_ref[0, rows, :], probe_ref[1, rows, :]
-            o_re, o_im = patch[0, rows, :], patch[1, rows, :]
+            o_re, o_im = patch[n, 0, rows, :].astype(F32), patch[n, 1, rows, :].astype(F32)
             steps = (p_re * re + p_im * im, p_re * im - p_im * re)
             for plane in range(2):
-                pieces = [steps[plane][:, t * LANES : (t + 1) * LANES] for t in range(tiles)]
+                pieces = [tile_of(steps[plane], t) for t in range(tiles)]
                 rolled = [turned(piece) for piece in pieces]
                 zero = jnp.zeros_like(pieces[0])
                 moved = []
@@ -186,16 +200,28 @@
                     before = rolled[t - 1] if t > 0 else zero
                     here = rolled[t] if t < tiles else zero
                     moved.append(
-                        jnp.where(odd, jnp.where(low, before, here), pieces[t] if t < tiles else zero)
+                        jnp.where(odd[n], jnp.where(low, before, here), pieces[t] if t < tiles else zero)
                     )
-                where = (plane, pl.ds(pl.multiple_of(row + start, CHUNK), CHUNK), pl.ds(base, frame + LANES))
-                total[where] += jnp.concatenate(moved, axis=1)
+                total[window(n, plane, start)] += jnp.concatenate(moved, axis=1)
             grads[0, rows, :] += o_re * re + o_im * im
             grads[1, rows, :] += o_re * im - o_im * re
-            grads[2, rows, :] += o_re * o_re + o_im * o_im
-        return carry
-
-    lax.fori_loop(0, count_ref[0], one, 0)
+            grads[2, rows, :] += (o_re * o_re + o_im * o_im) * live[n]
+
+    stages = (
+        exit_wave,
+        lambda n: left_product(n, plus_ref),
+        lambda n: right_product(n, minus_ref),
+        change,
+        lambda n: left_product(n, minus_ref),
+        lambda n: right_product(n, plus_ref),
+        update,
+    )
+    groups = [range(n, min(n + GROUP, count)) for n in range(0, count, GROUP)]
+    for time in range(len(stages) + STAGGER * (len(groups) - 1)):
+        for place in reversed(range(len(groups))):
+            if 0 <= time - STAGGER * place < len(stages):
+                for n in groups[place]:
+                    stages[time - STAGGER * place](n)
 
     part_frame = frame // 2
     for who, l_ref, r_ref, g_ref in ((1 - mode, lsend_ref, rsend_ref, gsend_ref), (mode, lkeep_ref, rkeep_ref, gkeep_ref)):
@@ -307,6 +333,34 @@
 def swapped(value, axis, distance):
     count = lax.axis_size(axis)
     return lax.ppermute(value, axis, [(source, source ^ distance) for source in range(count)])
+
+
+def frames(row_offset, col_offset, counts, own, pieces, probe, amplitudes, plus, minus):
+    _, tile_rows, tile_cols = own.shape
+    frame = probe.shape[1]
+    halo = frame - STEP
+    held = (tile_rows + halo) // 2
+    count = amplitudes.shape[0]
+    l_shape = shape((2, held, tile_cols), F32)
+    r_shape = shape((2, held * 3 // 2, LANES), F32)
+    g_shape = shape((3, frame // 2, frame), F32)
+    return vmem_call(
+        frames_kernel,
+        (l_shape, l_shape, r_shape, r_shape, g_shape, g_shape, shape((8, LANES), F32)),
+        row_offset, col_offset, counts, own, *pieces, probe, amplitudes, plus, minus,
+        smem=3,
+        scratch=[
+            pltpu.VMEM((2, tile_rows + halo, tile_cols + frame), BF16),
+            pltpu.VMEM((count, 2, frame, frame), BF16),
+            pltpu.VMEM((count, 2 * frame, frame), BF16),
+            pltpu.VMEM((count, frame, 2 * frame), BF16),
+            pltpu.VMEM((count, frame, 2 * frame), F32),
+            pltpu.VMEM((2, tile_rows + halo, tile_cols + frame), F32),
+            pltpu.VMEM((3, frame, frame), F32),
+        ],
+        flops=4 * 32 * frame**3,
+        name="frames",
+    )
 
 
 def body(object_field, probe_field, amplitudes, row_offset, col_offset, counts):
@@ -338,28 +392,11 @@
     own = planar(object_field)
     probe = jnp.transpose(probe_field, (1, 0, 2))
 
+    pieces = (r_mine, r_other, x_mine, x_other, d_mine, d_other)
+    lkeep, lsend, rkeep, rsend, gkeep, gsend, peak = frames(
+        row_offset, col_offset, counts, own, pieces, probe, amplitudes, plus, minus
+    )
     held = mid + part
-    l_shape = shape((2, held, tile_cols), F32)
-    r_shape = shape((2, held * 3 // 2, LANES), F32)
-    g_shape = shape((3, frame // 2, frame), F32)
-    lkeep, lsend, rkeep, rsend, gkeep, gsend, peak = vmem_call(
-        frames_kernel,
-        (l_shape, l_shape, r_shape, r_shape, g_shape, g_shape, shape((8, LANES), F32)),
-        row_offset, col_offset, counts, own, r_mine, r_other, x_mine, x_other, d_mine, d_other,
-        probe, amplitudes, plus, minus,
-        smem=3,
-        scratch=[
-            pltpu.VMEM((2, tile_rows + halo, tile_cols + frame), BF16),
-            pltpu.VMEM((2, frame, frame), F32),
-            pltpu.VMEM((2 * frame, frame), BF16),
-            pltpu.VMEM((frame, 2 * frame), BF16),
-            pltpu.VMEM((frame, 2 * frame), F32),
-            pltpu.VMEM((2, tile_rows + halo, tile_cols + frame), F32),
-            pltpu.VMEM((3, frame, frame), F32),
-        ],
-        flops=4 * 32 * frame**3,
-        name="frames",
-    )
     rrecv = swapped(rsend, "mode", 1)
     grecv = swapped(gsend, "mode", 1)
     rrecv, grecv, lsend = lax.optimization_barrier((rrecv, grecv, lsend))

time: 58.6 us -> 55 us (0.939); the launches traced: 59.2 us -> 54.7 us
  Pallas kernels: 11.5 us -> 7.88 us
  starting transfers between devices: 17.8 us -> 17.1 us
    pallas_call x9, Pallas kernels: 11.5 us -> 7.88 us  [vmem_call(): pl.pallas_call(kernel, out_shape=tuple((jax.ShapeDtypeStruct(o.shape, o.d...]
    ppermute x15, starting transfers between devices: 10.4 us -> 9.8 us  [swapped(): lax.ppermute(value, axis, [(source, source ^ distance) for source in rang...]
  transfers between devices with their start and end apart: 18 -> 18, of which waited for: 10 -> 9; matrix products, arithmetic and copies ran while one was open for 0% -> 0% of each run, Pallas kernels for 3% -> 3%
where the time goes in v1:
time: 55 us; the launch traced here: 54.7 us
  waiting for transfers between devices  26 us (47%)
  starting transfers between devices  17.1 us (31%)
  Pallas kernels  7.88 us (14%)
  local copies, waits for them, and re-layouts  2.25 us (4%)
  between operations  1.51 us (3%)
    ppermute x15, waiting for transfers between devices, swapped(): lax.ppermute(value, axis, [(source, source ^ distance) for source in rang...  18.6 us
    ppermute x15, starting transfers between devices, swapped(): lax.ppermute(value, axis, [(source, source ^ distance) for source in rang...  9.8 us
    pallas_call x9, Pallas kernels, vmem_call(): pl.pallas_call(kernel, out_shape=tuple((jax.ShapeDtypeStruct(o.shape, o.d...  7.88 us
    ppermute x1, waiting for transfers between devices, body(): d_mine = lax.ppermute(d_send, ('row', 'col'), diagonal)  7.41 us
    ppermute x2, starting transfers between devices, moved_along(): lax.ppermute(value, axis, [(source, source + steps) for source in range(f...  6.04 us
    unnamed x16, local copies, waits for them, and re-layouts  2.18 us
    ppermute x1, starting transfers between devices, body(): d_mine = lax.ppermute(d_send, ('row', 'col'), diagonal)  1.29 us
  transfers between devices with their start and end apart: 18, of which 9 were waited for; matrix products, arithmetic and copies ran while one was open for 0% of the time, Pallas kernels for 3%

profile of v1, /device:TPU:0, one launch (start us, length us, event | category | flops | bytes accessed | tf_op | source)
XLA Modules:
  0.0 54.7 jit_solution(1863615382013741027)
XLA Ops:
  0.6 1.4 %copy.18 = bf16[256,2,512]{2,0,1:T(8,128)(2,1)S(1)} copy(f32[256,2,512]{2,1,0:T(2,128)} %object_ref.1) | data formatting | bytes 1572864 | tf_op args[0]
  2.0 0.0 copy-start.6
  2.1 0.0 copy-start.1
  2.1 1.4 %collective-permute-start = (bf16[2,96,512]{2,1,0:T(8,128)(2,1)S(1)}, bf16[2,96,512]{2,1,0:T(8,128)(2,1)S(1)}, u32[]{:S(2)}, u32[]{:S(2)}) collective-permute-start(bf16[2,96,512]{2,1,0:T(8,128)(2,1)S(1)} %fusion), channel_id=1, source_target_pairs={{4,0},{8,4},{12,8},{5,1},{9,5},{13,9},{6,2},{10,6},{14,10},{7,3},{... | collective-permute-start | bytes 589832 | tf_op jit(solution)/shard_map/ppermute | solution.py:330
  3.6 3.0 %collective-permute-start.2 = (bf16[2,128,256]{2,1,0:T(8,128)(2,1)S(1)}, bf16[2,128,256]{2,1,0:T(8,128)(2,1)S(1)}, u32[]{:S(2)}, u32[]{:S(2)}) collective-permute-start(bf16[2,128,256]{2,1,0:T(8,128)(2,1)S(1)} %fusion.1), channel_id=1, source_target_pairs={{0,2},{2,0},{1,3},{3,1},{4,6},{6,4},{5,7},{7,5},{8,10},{10,8},{9,1... | collective-permute-start | bytes 393224 | tf_op jit(solution)/shard_map/ppermute | solution.py:335
  6.6 1.3 %collective-permute-start.1 = (bf16[2,96,256]{2,1,0:T(8,128)(2,1)S(1)}, bf16[2,96,256]{2,1,0:T(8,128)(2,1)S(1)}, u32[]{:S(2)}, u32[]{:S(2)}) collective-permute-start(bf16[2,96,256]{2,1,0:T(8,128)(2,1)S(1)} %slice.7), channel_id=1, source_target_pairs={{6,0},{10,4},{14,8},{7,1},{11,5},{15,9},{22,16},{26,20},{30,24},{2... | collective-permute-start | bytes 294920 | tf_op jit(solution)/shard_map/ppermute | solution.py:388
  7.9 7.4 %collective-permute-done.1.d_mine = bf16[2,96,256]{2,1,0:T(8,128)(2,1)S(1)} collective-permute-done((bf16[2,96,256]{2,1,0:T(8,128)(2,1)S(1)}, bf16[2,96,256]{2,1,0:T(8,128)(2,1)S(1)}, u32[]{:S(2)}, u32[]{:S(2)}) %collective-permute-start.1) | collective-permute-done | bytes 98336 | tf_op jit(solution)/shard_map/ppermute | solution.py:388
  15.3 0.0 collective-permute-done.2.x_mine
  15.3 0.0 collective-permute-done.r_mine
  15.3 0.0 collective-permute-start.3
  15.3 0.5 collective-permute-start.4
  15.8 0.1 collective-permute-start.5
  16.5 0.0 copy-done.1
  16.5 0.0 copy-start.2
  16.5 0.0 copy-start.5
  16.6 0.5 collective-permute-done.5.d_other
  17.1 0.0 collective-permute-done.4.x_other
  17.1 0.0 collective-permute-done.3.r_other
  17.1 0.0 copy-start.3
  17.1 0.0 copy-start.4
  17.1 0.0 copy-done.6
  17.1 0.4 copy-done.2
  17.6 0.2 copy-done.5
  17.7 0.1 copy-done.3
  17.8 0.0 copy-done.4
  17.9 4.8 %frames.1 = (f32[2,224,512]{2,1,0:T(8,128)S(1)}, f32[2,224,512]{2,1,0:T(8,128)S(1)}, f32[2,336,128]{2,1,0:T(8,128)S(1)}, f32[2,336,128]{2,1,0:T(8,128)S(1)}, f32...) custom-call(s32[4]{0:T(128)S(1)} %copy-done.3, s32[4]{0:T(128)S(1)} %copy-done.4, ...), custom_call_target="tpu_custom_call" | custom-call | flops 2147483648 | bytes 6787108 | tf_op jit(solution)/shard_map/frames/pallas_call | solution.py:43
  22.7 0.4 collective-permute-start.7
  23.0 0.2 collective-permute-start.6
  23.3 1.7 %collective-permute-done.6.rrecv = f32[2,336,128]{2,1,0:T(8,128)S(1)} collective-permute-done((f32[2,336,128]{2,1,0:T(8,128)S(1)}, f32[2,336,128]{2,1,0:T(8,128)S(1)}, u32[]{:S(2)}, u32[]{:S(2)}) %collective-permute-start.6) | collective-permute-done | bytes 344096 | tf_op jit(solution)/shard_map/ppermute | solution.py:335
  25.0 0.0 collective-permute-done.7.grecv
  25.0 0.3 collective-permute-start.8
  25.3 0.2 after_mode.1
  25.5 0.1 collective-permute-start.9
  25.6 1.7 %collective-permute-start.10 = (s16[272,256]{1,0:T(8,128)(2,1)S(1)}, s16[272,256]{1,0:T(8,128)(2,1)S(1)}, u32[]{:S(2)}, u32[]{:S(2)}) collective-permute-start(s16[272,256]{1,0:T(8,128)(2,1)S(1)} %get-tuple-element.54), channel_id=1, source_target_pairs={{0,4},{4,0},{8,12},{12,8},{1,5},{5,1},{9,13},{13,9},{2,6},{6,2},{1... | collective-permute-start | bytes 417800 | tf_op jit(solution)/shard_map/ppermute | solution.py:335
  27.2 1.1 %collective-permute-start.11 = (s16[144,256]{1,0:T(8,128)(2,1)S(1)}, s16[144,256]{1,0:T(8,128)(2,1)S(1)}, u32[]{:S(2)}, u32[]{:S(2)}) collective-permute-start(s16[144,256]{1,0:T(8,128)(2,1)S(1)} %get-tuple-element.56), channel_id=1, source_target_pairs={{0,8},{4,12},{8,0},{12,4},{1,9},{5,13},{9,1},{13,5},{2,10},{6,14},... | collective-permute-start | bytes 221192 | tf_op jit(solution)/shard_map/ppermute | solution.py:335
  28.3 4.2 %collective-permute-done.11.wrecv = s16[144,256]{1,0:T(8,128)(2,1)S(1)} collective-permute-done((s16[144,256]{1,0:T(8,128)(2,1)S(1)}, s16[144,256]{1,0:T(8,128)(2,1)S(1)}, u32[]{:S(2)}, u32[]{:S(2)}) %collective-permute-start.11) | collective-permute-done | bytes 73760 | tf_op jit(solution)/shard_map/ppermute | solution.py:335
  32.5 0.5 collective-permute-done.10.grecv
  33.0 0.1 joined.1
  33.2 0.0 collective-permute-done.9.xrecv
  33.2 0.0 collective-permute-done.8.lrecv
  33.2 0.0 copy-start
  33.2 0.2 from_left.1
  33.4 4.6 %collective-permute-start.12 = (s16[208,512]{1,0:T(8,128)(2,1)S(1)}, s16[208,512]{1,0:T(8,128)(2,1)S(1)}, u32[]{:S(2)}, u32[]{:S(2)}) collective-permute-start(s16[208,512]{1,0:T(8,128)(2,1)S(1)} %get-tuple-element.60), channel_id=1, source_target_pairs={{0,4},{4,8},{8,12},{1,5},{5,9},{9,13},{2,6},{6,10},{10,14},{3,7},{... | collective-permute-start | bytes 638984 | tf_op jit(solution)/shard_map/ppermute | solution.py:330
  38.0 1.7 %collective-permute-start.13 = (s16[400,256]{1,0:T(8,128)(2,1)S(1)}, s16[400,256]{1,0:T(8,128)(2,1)S(1)}, u32[]{:S(2)}, u32[]{:S(2)}) collective-permute-start(s16[400,256]{1,0:T(8,128)(2,1)S(1)} %get-tuple-element.62), channel_id=1, source_target_pairs={{0,2},{2,0},{1,3},{3,1},{4,6},{6,4},{5,7},{7,5},{8,10},{10,8},{9,1... | collective-permute-start | bytes 614408 | tf_op jit(solution)/shard_map/ppermute | solution.py:335
  39.8 4.4 %collective-permute-done.13.recv = s16[400,256]{1,0:T(8,128)(2,1)S(1)} collective-permute-done((s16[400,256]{1,0:T(8,128)(2,1)S(1)}, s16[400,256]{1,0:T(8,128)(2,1)S(1)}, u32[]{:S(2)}, u32[]{:S(2)}) %collective-permute-start.13) | collective-permute-done | bytes 204832 | tf_op jit(solution)/shard_map/ppermute | solution.py:335
  44.1 0.1 split.1
  44.3 0.4 collective-permute-start.15
  44.7 0.0 collective-permute-done.12.rowrecv
  44.7 0.1 from_above.1
  44.8 0.1 collective-permute-start.14
  44.9 0.2 collective-permute-start.16
  45.1 1.1 %collective-permute-done.14.spilled = f32[2,32,512]{2,1,0:T(8,128)S(1)} collective-permute-done((f32[2,32,512]{2,1,0:T(8,128)S(1)}, f32[2,32,512]{2,1,0:T(8,128)S(1)}, u32[]{:S(2)}, u32[]{:S(2)}) %collective-permute-start.14) | collective-permute-done | bytes 131104 | tf_op jit(solution)/shard_map/ppermute | solution.py:335
  46.2 0.0 copy-done
  46.2 1.1 %object.1 = f32[128,2,512]{2,1,0:T(2,128)} custom-call(f32[256,2,512]{2,1,0:T(2,128)S(1)} %copy-done, f32[2,128,512]{2,1,0:T(8,128)S(1)} %get-tuple-element.59.tile, f32[2,96,512]{2,1,0:T(8,128)S(1)} %get-tuple-element.65.rows, f32[2,32,512]{2,1,0:T(8,128)S(1)} %collective-permute-done.14.spilled, f32[8,128]{1,0:T(8,128)S(1)} %get-tuple-element.67.peak), custom_call_target="tpu_custom_call" | custom-call | bytes 2625536 | tf_op jit(solution)/shard_map/object/pallas_call | solution.py:43
  47.3 4.6 %collective-permute-done.15.grecv = s16[272,256]{1,0:T(8,128)(2,1)S(1)} collective-permute-done((s16[272,256]{1,0:T(8,128)(2,1)S(1)}, s16[272,256]{1,0:T(8,128)(2,1)S(1)}, u32[]{:S(2)}, u32[]{:S(2)}) %collective-permute-start.15) | collective-permute-done | bytes 139296 | tf_op jit(solution)/shard_map/ppermute | solution.py:335
  51.9 0.0 collective-permute-done.16.wrecv
  51.9 0.1 probe.1.mine
  52.0 0.1 collective-permute-start.17
  52.1 1.5 %collective-permute-done.17.other = f32[2,128,256]{2,1,0:T(8,128)S(1)} collective-permute-done((f32[2,128,256]{2,1,0:T(8,128)S(1)}, f32[2,128,256]{2,1,0:T(8,128)S(1)}, u32[]{:S(2)}, u32[]{:S(2)}) %collective-permute-start.17) | collective-permute-done | bytes 262176 | tf_op jit(solution)/shard_map/ppermute | solution.py:335
  53.6 1.1 %probe_out.1 = f32[256,2,256]{2,1,0:T(2,128)} custom-call(f32[256,2,256]{2,1,0:T(2,128)S(1)} %copy-done.1, f32[2,128,256]{2,1,0:T(8,128)S(1)} %probe.1.mine, f32[2,128,256]{2,1,0:T(8,128)S(1)} %collective-permute-done.17.other), custom_call_target="tpu_custom_call" | custom-call | bytes 1572864 | tf_op jit(solution)/shard_map/probe_out/pallas_call | solution.py:43
  (5 shorter events, 0.1 us)
Async XLA Ops:
  2.0 15.1 %copy-start.6 = (bf16[512,512]{1,0:T(8,128)(2,1)S(1)}, bf16[512,512]{1,0:T(8,128)(2,1)}, u32[]{:S(2)}) copy-start(bf16[512,512]{1,0:T(8,128)(2,1)} %constant.16.clone.plus_ref) | copy-start | bytes 1572868
  2.1 14.5 %copy-start.1 = (f32[256,2,256]{2,1,0:T(2,128)S(1)}, f32[256,2,256]{2,1,0:T(2,128)}, u32[]{:S(2)}) copy-start(f32[256,2,256]{2,1,0:T(2,128)} %probe_ref.1) | copy-start | bytes 1572868
  2.1 13.2 %collective-permute-start = (bf16[2,96,512]{2,1,0:T(8,128)(2,1)S(1)}, bf16[2,96,512]{2,1,0:T(8,128)(2,1)S(1)}, u32[]{:S(2)}, u32[]{:S(2)}) collective-permute-start(bf16[2,96,512]{2,1,0:T(8,128)(2,1)S(1)} %fusion), channel_id=1, source_target_pairs={{4,0},{8,4},{12,8},{5,1},{9,5},{13,9},{6,2},{10,6},{14,10},{7,3},{... | collective-permute-start | bytes 589832 | tf_op jit(solution)/shard_map/ppermute | solution.py:330
  3.6 11.7 %collective-permute-start.2 = (bf16[2,128,256]{2,1,0:T(8,128)(2,1)S(1)}, bf16[2,128,256]{2,1,0:T(8,128)(2,1)S(1)}, u32[]{:S(2)}, u32[]{:S(2)}) collective-permute-start(bf16[2,128,256]{2,1,0:T(8,128)(2,1)S(1)} %fusion.1), channel_id=1, source_target_pairs={{0,2},{2,0},{1,3},{3,1},{4,6},{6,4},{5,7},{7,5},{8,10},{10,8},{9,1... | collective-permute-start | bytes 393224 | tf_op jit(solution)/shard_map/ppermute | solution.py:335
  6.6 8.7 %collective-permute-start.1 = (bf16[2,96,256]{2,1,0:T(8,128)(2,1)S(1)}, bf16[2,96,256]{2,1,0:T(8,128)(2,1)S(1)}, u32[]{:S(2)}, u32[]{:S(2)}) collective-permute-start(bf16[2,96,256]{2,1,0:T(8,128)(2,1)S(1)} %slice.7), channel_id=1, source_target_pairs={{6,0},{10,4},{14,8},{7,1},{11,5},{15,9},{22,16},{26,20},{30,24},{2... | collective-permute-start | bytes 294920 | tf_op jit(solution)/shard_map/ppermute | solution.py:388
  15.3 1.8 %collective-permute-start.3 = (bf16[2,96,512]{2,1,0:T(8,128)(2,1)S(1)}, bf16[2,96,512]{2,1,0:T(8,128)(2,1)S(1)}, u32[]{:S(2)}, u32[]{:S(2)}) collective-permute-start(bf16[2,96,512]{2,1,0:T(8,128)(2,1)S(1)} %collective-permute-done.r_mine), channel_id=1, source_target_pairs={{0,1},{1,0},{2,3},{3,2},{4,5},{5,4},{6,7},{7,6},{8,9},{9,8},{10,11... | collective-permute-start | bytes 589832 | tf_op jit(solution)/shard_map/ppermute | solution.py:335
  15.3 1.8 %collective-permute-start.4 = (bf16[2,128,256]{2,1,0:T(8,128)(2,1)S(1)}, bf16[2,128,256]{2,1,0:T(8,128)(2,1)S(1)}, u32[]{:S(2)}, u32[]{:S(2)}) collective-permute-start(bf16[2,128,256]{2,1,0:T(8,128)(2,1)S(1)} %collective-permute-done.2.x_mine), channel_id=1, source_target_pairs={{0,1},{1,0},{2,3},{3,2},{4,5},{5,4},{6,7},{7,6},{8,9},{9,8},{10,11... | collective-permute-start | bytes 393224 | tf_op jit(solution)/shard_map/ppermute | solution.py:335
  15.8 1.3 %collective-permute-start.5 = (bf16[2,96,256]{2,1,0:T(8,128)(2,1)S(1)}, bf16[2,96,256]{2,1,0:T(8,128)(2,1)S(1)}, u32[]{:S(2)}, u32[]{:S(2)}) collective-permute-start(bf16[2,96,256]{2,1,0:T(8,128)(2,1)S(1)} %collective-permute-done.1.d_mine), channel_id=1, source_target_pairs={{0,1},{1,0},{2,3},{3,2},{4,5},{5,4},{6,7},{7,6},{8,9},{9,8},{10,11... | collective-permute-start | bytes 294920 | tf_op jit(solution)/shard_map/ppermute | solution.py:335
  16.5 1.0 %copy-start.2 = (bf16[4,256,256]{2,1,0:T(8,128)(2,1)S(1)}, bf16[4,256,256]{2,1,0:T(8,128)(2,1)}, u32[]{:S(2)}) copy-start(bf16[4,256,256]{2,1,0:T(8,128)(2,1)} %amp_ref.1) | copy-start | bytes 1572868
  16.5 1.2 %copy-start.5 = (bf16[512,512]{1,0:T(8,128)(2,1)S(1)}, bf16[512,512]{1,0:T(8,128)(2,1)}, u32[]{:S(2)}) copy-start(bf16[512,512]{1,0:T(8,128)(2,1)} %constant.17.clone.minus_ref) | copy-start | bytes 1572868
  17.1 0.7 %copy-start.3 = (s32[4]{0:T(128)S(1)}, s32[4]{0:T(128)}, u32[]{:S(2)}) copy-start(s32[4]{0:T(128)} %row_ref.1) | copy-start | bytes 52
  17.1 0.7 %copy-start.4 = (s32[4]{0:T(128)S(1)}, s32[4]{0:T(128)}, u32[]{:S(2)}) copy-start(s32[4]{0:T(128)} %col_ref.1) | copy-start | bytes 52
  22.7 2.3 %collective-permute-start.7 = (f32[3,128,256]{2,1,0:T(8,128)S(1)}, f32[3,128,256]{2,1,0:T(8,128)S(1)}, u32[]{:S(2)}, u32[]{:S(2)}) collective-permute-start(f32[3,128,256]{2,1,0:T(8,128)S(1)} %get-tuple-element.45), channel_id=1, source_target_pairs={{0,1},{1,0},{2,3},{3,2},{4,5},{5,4},{6,7},{7,6},{8,9},{9,8},{10,11... | collective-permute-start | bytes 1179656 | tf_op jit(solution)/shard_map/ppermute | solution.py:335
  23.0 1.9 %collective-permute-start.6 = (f32[2,336,128]{2,1,0:T(8,128)S(1)}, f32[2,336,128]{2,1,0:T(8,128)S(1)}, u32[]{:S(2)}, u32[]{:S(2)}) collective-permute-start(f32[2,336,128]{2,1,0:T(8,128)S(1)} %get-tuple-element.44), channel_id=1, source_target_pairs={{0,1},{1,0},{2,3},{3,2},{4,5},{5,4},{6,7},{7,6},{8,9},{9,8},{10,11... | collective-permute-start | bytes 1032200 | tf_op jit(solution)/shard_map/ppermute | solution.py:335
  25.0 8.2 %collective-permute-start.8 = (f32[2,224,512]{2,1,0:T(8,128)S(1)}, f32[2,224,512]{2,1,0:T(8,128)S(1)}, u32[]{:S(2)}, u32[]{:S(2)}) collective-permute-start(f32[2,224,512]{2,1,0:T(8,128)S(1)} %get-tuple-element.47), channel_id=1, source_target_pairs={{0,1},{1,0},{2,3},{3,2},{4,5},{5,4},{6,7},{7,6},{8,9},{9,8},{10,11... | collective-permute-start | bytes 2752520 | tf_op jit(solution)/shard_map/ppermute | solution.py:335
  25.5 7.7 %collective-permute-start.9 = (s16[688,128]{1,0:T(8,128)(2,1)S(1)}, s16[688,128]{1,0:T(8,128)(2,1)S(1)}, u32[]{:S(2)}, u32[]{:S(2)}) collective-permute-start(s16[688,128]{1,0:T(8,128)(2,1)S(1)} %get-tuple-element.52), channel_id=1, source_target_pairs={{0,2},{2,0},{1,3},{3,1},{4,6},{6,4},{5,7},{7,5},{8,10},{10,8},{9,1... | collective-permute-start | bytes 528392 | tf_op jit(solution)/shard_map/ppermute | solution.py:335
  25.6 7.4 %collective-permute-start.10 = (s16[272,256]{1,0:T(8,128)(2,1)S(1)}, s16[272,256]{1,0:T(8,128)(2,1)S(1)}, u32[]{:S(2)}, u32[]{:S(2)}) collective-permute-start(s16[272,256]{1,0:T(8,128)(2,1)S(1)} %get-tuple-element.54), channel_id=1, source_target_pairs={{0,4},{4,0},{8,12},{12,8},{1,5},{5,1},{9,13},{13,9},{2,6},{6,2},{1... | collective-permute-start | bytes 417800 | tf_op jit(solution)/shard_map/ppermute | solution.py:335
  27.2 5.3 %collective-permute-start.11 = (s16[144,256]{1,0:T(8,128)(2,1)S(1)}, s16[144,256]{1,0:T(8,128)(2,1)S(1)}, u32[]{:S(2)}, u32[]{:S(2)}) collective-permute-start(s16[144,256]{1,0:T(8,128)(2,1)S(1)} %get-tuple-element.56), channel_id=1, source_target_pairs={{0,8},{4,12},{8,0},{12,4},{1,9},{5,13},{9,1},{13,5},{2,10},{6,14},... | collective-permute-start | bytes 221192 | tf_op jit(solution)/shard_map/ppermute | solution.py:335
  33.2 13.0 %copy-start = (f32[256,2,512]{2,1,0:T(2,128)S(1)}, f32[256,2,512]{2,1,0:T(2,128)}, u32[]{:S(2)}) copy-start(f32[256,2,512]{2,1,0:T(2,128)} %object_ref.1) | copy-start | bytes 3145732
  33.4 11.3 %collective-permute-start.12 = (s16[208,512]{1,0:T(8,128)(2,1)S(1)}, s16[208,512]{1,0:T(8,128)(2,1)S(1)}, u32[]{:S(2)}, u32[]{:S(2)}) collective-permute-start(s16[208,512]{1,0:T(8,128)(2,1)S(1)} %get-tuple-element.60), channel_id=1, source_target_pairs={{0,4},{4,8},{8,12},{1,5},{5,9},{9,13},{2,6},{6,10},{10,14},{3,7},{... | collective-permute-start | bytes 638984 | tf_op jit(solution)/shard_map/ppermute | solution.py:330
  38.0 6.1 %collective-permute-start.13 = (s16[400,256]{1,0:T(8,128)(2,1)S(1)}, s16[400,256]{1,0:T(8,128)(2,1)S(1)}, u32[]{:S(2)}, u32[]{:S(2)}) collective-permute-start(s16[400,256]{1,0:T(8,128)(2,1)S(1)} %get-tuple-element.62), channel_id=1, source_target_pairs={{0,2},{2,0},{1,3},{3,1},{4,6},{6,4},{5,7},{7,5},{8,10},{10,8},{9,1... | collective-permute-start | bytes 614408 | tf_op jit(solution)/shard_map/ppermute | solution.py:335
  44.3 7.6 %collective-permute-start.15 = (s16[272,256]{1,0:T(8,128)(2,1)S(1)}, s16[272,256]{1,0:T(8,128)(2,1)S(1)}, u32[]{:S(2)}, u32[]{:S(2)}) collective-permute-start(s16[272,256]{1,0:T(8,128)(2,1)S(1)} %get-tuple-element.68), channel_id=1, source_target_pairs={{0,8},{4,12},{8,0},{12,4},{1,9},{5,13},{9,1},{13,5},{2,10},{6,14},... | collective-permute-start | bytes 417800 | tf_op jit(solution)/shard_map/ppermute | solution.py:335
  44.8 1.4 %collective-permute-start.14 = (f32[2,32,512]{2,1,0:T(8,128)S(1)}, f32[2,32,512]{2,1,0:T(8,128)S(1)}, u32[]{:S(2)}, u32[]{:S(2)}) collective-permute-start(f32[2,32,512]{2,1,0:T(8,128)S(1)} %get-tuple-element.66), channel_id=1, source_target_pairs={{0,1},{1,0},{2,3},{3,2},{4,5},{5,4},{6,7},{7,6},{8,9},{9,8},{10,11... | collective-permute-start | bytes 393224 | tf_op jit(solution)/shard_map/ppermute | solution.py:335
  44.9 7.1 %collective-permute-start.16 = (s16[144,256]{1,0:T(8,128)(2,1)S(1)}, s16[144,256]{1,0:T(8,128)(2,1)S(1)}, u32[]{:S(2)}, u32[]{:S(2)}) collective-permute-start(s16[144,256]{1,0:T(8,128)(2,1)S(1)} %get-tuple-element.73), channel_id=1, source_target_pairs={{0,4},{4,0},{8,12},{12,8},{1,5},{5,1},{9,13},{13,9},{2,6},{6,2},{1... | collective-permute-start | bytes 221192 | tf_op jit(solution)/shard_map/ppermute | solution.py:335
  52.0 1.6 %collective-permute-start.17 = (f32[2,128,256]{2,1,0:T(8,128)S(1)}, f32[2,128,256]{2,1,0:T(8,128)S(1)}, u32[]{:S(2)}, u32[]{:S(2)}) collective-permute-start(f32[2,128,256]{2,1,0:T(8,128)S(1)} %probe.1.mine), channel_id=1, source_target_pairs={{0,1},{1,0},{2,3},{3,2},{4,5},{5,4},{6,7},{7,6},{8,9},{9,8},{10,11... | collective-permute-start | bytes 786440 | tf_op jit(solution)/shard_map/ppermute | solution.py:335

commit v2 on v1

--- a/solution.py
+++ b/solution.py
@@ -14,6 +14,7 @@
 STEP = 64
 LANES = 128
 PAD = 16
+WTAIL = 272
 BITS = 14
 CHUNK = 32
 GROUP = 2
@@ -36,16 +37,16 @@
     return jnp.asarray(plus, BF16), jnp.asarray(minus, BF16)
 
 
-def vmem_call(kernel, outs, *operands, smem=0, scratch=(), flops=0, name=None):
-    specs = [pl.BlockSpec(memory_space=pltpu.SMEM)] * smem
-    specs += [pl.BlockSpec(memory_space=pltpu.VMEM)] * (len(operands) - smem)
+def vmem_call(kernel, outs, *operands, smem=0, far=(), far_out=False, into=None, scratch=(), flops=0, name=None):
+    places = [pltpu.SMEM if n < smem else pltpu.HBM if n in far else pltpu.VMEM for n in range(len(operands))]
     moved = sum(math.prod(o.shape) * o.dtype.itemsize for o in (*operands, *outs))
     return pl.pallas_call(
         kernel,
         out_shape=tuple(jax.ShapeDtypeStruct(o.shape, o.dtype) for o in outs),
-        in_specs=specs,
-        out_specs=tuple(pl.BlockSpec(memory_space=pltpu.VMEM) for _ in outs),
+        in_specs=[pl.BlockSpec(memory_space=place) for place in places],
+        out_specs=tuple(pl.BlockSpec(memory_space=pltpu.HBM if far_out else pltpu.VMEM) for _ in outs),
         scratch_shapes=scratch,
+        input_output_aliases={} if into is None else {into: 0},
         compiler_params=pltpu.CompilerParams(vmem_limit_bytes=40 * 1024 * 1024),
         cost_estimate=pl.CostEstimate(flops=flops, bytes_accessed=moved, transcendentals=0),
         name=name,
@@ -63,27 +64,43 @@
     return whole.astype(jnp.int32).astype(I16), power, whole * jnp.exp2(power - BITS)
 
 
-def encode_to(ref, blocks):
-    rows, cols = blocks[0].shape
-    tail = jnp.zeros((PAD, cols), F32)
-    row = lax.broadcasted_iota(jnp.int32, (PAD, cols), 0)
-    decoded = []
-    for n, block in enumerate(blocks):
-        code, power, back = encode(block)
-        ref[n * rows : (n + 1) * rows, :] = code
-        tail = jnp.where(row == n, power, tail)
-        decoded.append(back)
-    ref[len(blocks) * rows :, :] = tail.astype(jnp.int32).astype(I16)
+def tile_of(value, tile):
+    return value[:, tile * LANES : (tile + 1) * LANES]
+
+
+def code_shape(planes, rows, cols, tail=PAD):
+    return shape((planes * rows * cols // LANES + tail, LANES), I16)
+
+
+def encode_to(ref, planes):
+    rows, cols = planes[0].shape
+    tail = jnp.zeros((PAD, LANES), F32)
+    row = lax.broadcasted_iota(jnp.int32, (PAD, LANES), 0)
+    decoded, n = [], 0
+    for plane in planes:
+        blocks = []
+        for tile in range(cols // LANES):
+            code, power, back = encode(tile_of(plane, tile))
+            ref[n * rows : (n + 1) * rows, :] = code
+            tail = jnp.where(row == n, power, tail)
+            blocks.append(back)
+            n += 1
+        decoded.append(jnp.concatenate(blocks, axis=1))
+    ref[n * rows : n * rows + PAD, :] = tail.astype(jnp.int32).astype(I16)
+    if ref.shape[0] > n * rows + PAD:
+        ref[n * rows + PAD :, :] = jnp.zeros((ref.shape[0] - n * rows - PAD, LANES), I16)
     return decoded
 
 
-def decode(ref, count):
-    rows = (ref.shape[0] - PAD) // count
-    tail = ref[count * rows :, :].astype(jnp.int32).astype(F32)
-    return [
+def decode(ref, planes, rows, cols):
+    tiles = cols // LANES
+    first = planes * tiles * rows
+    tail = ref[first : first + PAD, :].astype(jnp.int32).astype(F32)
+    blocks = [
         ref[n * rows : (n + 1) * rows, :].astype(jnp.int32).astype(F32) * jnp.exp2(tail[n : n + 1] - BITS)
-        for n in range(count)
+        for n in range(planes * tiles)
     ]
+    return [jnp.concatenate(blocks[n * tiles : (n + 1) * tiles], axis=1) for n in range(planes)]
 
 
 def turned(value):
@@ -125,8 +142,9 @@
     for who, below, right, diagonal in ((mode, r_mine, x_mine, d_mine), (1 - mode, r_other, x_other, d_other)):
         rows = pl.ds(pl.multiple_of(tile_rows + who * part, 32), part)
         ext[:, rows, :tile_cols] = below[...]
-        ext[:, rows, tile_cols:] = diagonal[...]
-        ext[:, pl.ds(pl.multiple_of(who * mid, mid), mid), tile_cols:] = right[...]
+        for plane in range(2):
+            ext[plane, rows, tile_cols:] = unfolded(diagonal[plane].astype(F32)).astype(BF16)
+        ext[:, pl.ds(pl.multiple_of(who * mid, mid), mid), tile_cols : tile_cols + right.shape[2]] = right[...]
 
     power = probe_ref[0] * probe_ref[0] + probe_ref[1] * probe_ref[1]
     peak_ref[...] = jnp.broadcast_to(jnp.max(power, keepdims=True), peak_ref.shape) + EPSILON
@@ -146,9 +164,6 @@
     def window(n, plane, start):
         rows = pl.ds(pl.multiple_of(base_row[n] + start, CHUNK), CHUNK)
         return plane, rows, pl.ds(base_col[n], frame + LANES)
-
-    def tile_of(value, t):
-        return value[:, t * LANES : (t + 1) * LANES]
 
     def exit_wave(n):
         for start in range(0, frame, CHUNK):
@@ -243,19 +258,19 @@
 
 
 def joined_kernel(g, grecv, w, wrecv, sums_ref, send_ref):
-    got = decode(grecv, 2)
-    sums = [g[plane] + got[plane] for plane in range(2)] + [w[...] + decode(wrecv, 1)[0]]
+    got = decode(grecv, 2, *w.shape) + decode(wrecv, 1, *w.shape)
+    sums = [g[0] + got[0], g[1] + got[1], w[...] + got[2]]
     sums_ref[0], sums_ref[1], sums_ref[2] = encode_to(send_ref, sums)
 
 
 def split_kernel(sums, recv, g_ref, gsend_ref, w_ref, wsend_ref):
-    total = [sums[plane] + got for plane, got in enumerate(decode(recv, 3))]
+    total = [sums[plane] + got for plane, got in enumerate(decode(recv, 3, *sums.shape[1:]))]
     g_ref[0], g_ref[1] = encode_to(gsend_ref, total[:2])
     (w_ref[...],) = encode_to(wsend_ref, total[2:])
 
 
 def again_kernel(sums, recv, sums_ref, send_ref):
-    total = [sums[plane] + got for plane, got in enumerate(decode(recv, 3))]
+    total = [sums[plane] + got for plane, got in enumerate(decode(recv, 3, *sums.shape[1:]))]
     sums_ref[0], sums_ref[1], sums_ref[2] = encode_to(send_ref, total)
 
 
@@ -263,7 +278,7 @@
     rows = tile_ref.shape[1]
     came = jnp.where(lax.axis_index("col") > 0, 1.0, 0.0)
     below = []
-    for plane, code in enumerate(decode(xrecv, 2)):
+    for plane, code in enumerate(decode(xrecv, 2, lkeep.shape[1] * 3 // 2, LANES)):
         got = unfolded(code) * came
         frame = got.shape[1]
         tile_ref[plane, :, :frame] = lkeep[plane, :rows, :frame] + lrecv[plane, :rows, :frame] + got[:rows]
@@ -275,7 +290,7 @@
 
 
 def from_above_kernel(rowrecv, rows_ref, spill_ref):
-    got = decode(rowrecv, 2)
+    got = decode(rowrecv, 2, *rows_ref.shape[1:])
     came = jnp.where(lax.axis_index("row") > 0, 1.0, 0.0)
     over = spill_ref.shape[1]
     for plane in range(2):
@@ -304,22 +319,29 @@
 
 
 def probe_kernel(g, grecv, w, wrecv, step_ref):
-    weight = w[...] + decode(wrecv, 1)[0] + REGULARIZER
-    got = decode(grecv, 2)
+    weight = w[...] + decode(wrecv, 1, *w.shape)[0] + REGULARIZER
+    got = decode(grecv, 2, *w.shape)
     for plane in range(2):
         step_ref[plane] = (g[plane] + got[plane]) / weight
 
 
-def probe_out_kernel(probe_ref, mine, other, out_ref):
-    mode = lax.axis_index("mode")
-    rows = mine.shape[1]
-    for start in range(0, rows, CHUNK):
-        for plane in range(2):
-            one, two = mine[plane, start : start + CHUNK, :], other[plane, start : start + CHUNK, :]
-            first, second = jnp.where(mode == 0, one, two), jnp.where(mode == 0, two, one)
-            for place, step in ((start, first), (rows + start, second)):
-                old = probe_ref[place : place + CHUNK, plane, :]
-                out_ref[place : place + CHUNK, plane, :] = old + step
+def put_half(who, probe_ref, step, out_ref, block, arrived):
+    rows = step.shape[1]
+    place = pl.ds(pl.multiple_of(who * rows, rows), rows)
+    for plane in range(2):
+        block[:, plane, :] = probe_ref[place, plane, :] + step[plane]
+    copy = pltpu.make_async_copy(block, out_ref.at[place], arrived)
+    copy.start()
+    copy.wait()
+
+
+def probe_mine_kernel(probe_ref, step, out_ref, block, arrived):
+    put_half(lax.axis_index("mode"), probe_ref, step, out_ref, block, arrived)
+
+
+def probe_other_kernel(probe_ref, step, before_ref, out_ref, block, arrived):
+    del before_ref
+    put_half(1 - lax.axis_index("mode"), probe_ref, step, out_ref, block, arrived)
 
 
 def moved_along(value, axis, steps):
@@ -376,9 +398,13 @@
         return jnp.transpose(block.astype(BF16), (1, 0, 2))
 
     r_send = planar(lax.dynamic_slice_in_dim(object_field, mode * part, part, 0))
-    x_send = planar(lax.dynamic_slice_in_dim(object_field[:, :, :frame], mode * mid, mid, 0))
-    r_send, x_send = lax.optimization_barrier((r_send, x_send))
-    d_send = r_send[:, :, :frame]
+    corner = r_send[:, :, :halo]
+    thin = corner[:, :, LANES:]
+    thin = jnp.concatenate([thin[:, : part // 2], thin[:, part // 2 :]], axis=2)
+    d_send = jnp.concatenate([corner[:, :, :LANES], thin], axis=1)
+    object_later, r_send, d_send = lax.optimization_barrier((object_field, r_send, d_send))
+    x_send = planar(lax.dynamic_slice_in_dim(object_later[:, :, :halo], mode * mid, mid, 0))
+    x_send, x_last = lax.optimization_barrier((x_send[:1], x_send[1:]))
     diagonal = []
     for r in range(1, rows_count):
         for c in range(1, cols_count):
@@ -386,10 +412,11 @@
             diagonal.append((here, here - cols_count - 1))
     r_mine = moved_along(r_send, "row", -1)
     d_mine = lax.ppermute(d_send, ("row", "col"), diagonal)
-    x_mine = moved_along(x_send, "col", -1)
-    r_mine, d_mine, x_mine = lax.optimization_barrier((r_mine, d_mine, x_mine))
+    x_mine, x_last = moved_along(x_send, "col", -1), moved_along(x_last, "col", -1)
+    r_mine, d_mine, x_mine, x_last = lax.optimization_barrier((r_mine, d_mine, x_mine, x_last))
+    x_mine = jnp.concatenate([x_mine, x_last], axis=0)
     r_other, d_other, x_other = (swapped(v, "mode", 1) for v in (r_mine, d_mine, x_mine))
-    own = planar(object_field)
+    own = planar(object_later)
     probe = jnp.transpose(probe_field, (1, 0, 2))
 
     pieces = (r_mine, r_other, x_mine, x_other, d_mine, d_other)
@@ -403,14 +430,14 @@
     lrecv = swapped(lsend, "mode", 1)
 
     quarter = frame // 2
-    g_out = (shape((2, quarter, frame), F32), shape((2 * quarter + PAD, frame), I16))
-    w_out = (shape((quarter, frame), F32), shape((quarter + PAD, frame), I16))
-    all_out = (shape((3, quarter, frame), F32), shape((3 * quarter + PAD, frame), I16))
+    g_out = (shape((2, quarter, frame), F32), code_shape(2, quarter, frame))
+    w_out = (shape((quarter, frame), F32), code_shape(1, quarter, frame))
+    all_out = (shape((3, quarter, frame), F32), code_shape(3, quarter, frame))
     row_steps = [("row", 1 << k) for k in range(rows_count.bit_length() - 1)]
     col_steps = [("col", 1 << k) for k in range(cols_count.bit_length() - 1)]
 
     xsend, g, gcode, w, wcode = vmem_call(
-        after_mode_kernel, (shape((held * 3 + PAD, LANES), I16), *g_out, *w_out),
+        after_mode_kernel, (code_shape(2, held * 3 // 2, LANES), *g_out, *w_out),
         rkeep, rrecv, gkeep, grecv, name="after_mode",
     )
     xrecv = moved_along(xsend, "col", 1)
@@ -420,14 +447,16 @@
     came = swapped(code, *col_steps[0])
     tile, rowsend = vmem_call(
         from_left_kernel,
-        (shape((2, mid, tile_cols), F32), shape((2 * part + PAD, tile_cols), I16)),
+        (shape((2, mid, tile_cols), F32), code_shape(2, part, tile_cols)),
         lkeep, lrecv, xrecv, name="from_left",
     )
     rowrecv = moved_along(rowsend, "row", 1)
     for step in row_steps[2:] + col_steps[1:]:
         sums, code = vmem_call(again_kernel, all_out, sums, came, name="again")
         came = swapped(code, *step)
-    g, gcode, w, wcode = vmem_call(split_kernel, (*g_out, *w_out), sums, came, name="split")
+    g, gcode, w, wcode = vmem_call(
+        split_kernel, (*g_out, w_out[0], code_shape(1, quarter, frame, tail=WTAIL)), sums, came, name="split"
+    )
     gother, wother = swapped(gcode, *row_steps[1]), swapped(wcode, *row_steps[0])
 
     rowrecv, w = lax.optimization_barrier((rowrecv, w))
@@ -442,8 +471,14 @@
     object_new, gother = lax.optimization_barrier((object_new, gother))
     (step,) = vmem_call(probe_kernel, (shape((2, quarter, frame), F32),), g, gother, w, wother, name="probe")
     other = swapped(step, "mode", 1)
+    out = (shape(probe_field.shape, F32),)
+    scratch = [pltpu.VMEM((quarter, 2, frame), F32), pltpu.SemaphoreType.DMA]
+    (half_new,) = vmem_call(
+        probe_mine_kernel, out, probe_field, step, far_out=True, scratch=scratch, name="probe_mine"
+    )
     (probe_new,) = vmem_call(
-        probe_out_kernel, (shape(probe_field.shape, F32),), probe_field, step, other, name="probe_out"
+        probe_other_kernel, out, probe_field, other, half_new,
+        far=(2,), far_out=True, into=2, scratch=scratch, name="probe_other",
     )
     return (object_new, probe_new)
 

time: 55 us -> 50.2 us (0.913)
  waiting for transfers between devices: 26 us -> 15.5 us
  starting transfers between devices: 17.1 us -> 21.9 us
  Pallas kernels: 7.88 us -> 8.67 us
    ppermute x1, waiting for transfers between devices: 7.41 us -> 0.01 us  [body(): d_mine = lax.ppermute(d_send, ('row', 'col'), diagonal)]
    ppermute x15 -> x16, waiting for transfers between devices: 18.6 us -> 13.8 us  [swapped(): lax.ppermute(value, axis, [(source, source ^ distance) for source in rang...]
    ppermute x15 -> x16, starting transfers between devices: 9.8 us -> 14.6 us  [swapped(): lax.ppermute(value, axis, [(source, source ^ distance) for source in rang...]
    ppermute x2, waiting for transfers between devices: 0.01 us -> 1.73 us  [moved_along(): lax.ppermute(value, axis, [(source, source + steps) for source in range(f...]
    unnamed x16 -> x17, local copies, waits for them, and re-layouts: 2.18 us -> 0.81 us
    dynamic_slice x0 -> x1, local copies, waits for them, and re-layouts: none -> 1.22 us  [body(): lax.dynamic_slice_in_dim(object_field, mode * part, part, 0)]
    pallas_call x9 -> x10, Pallas kernels: 7.88 us -> 8.67 us  [vmem_call(): pl.pallas_call(kernel, out_shape=tuple((jax.ShapeDtypeStruct(o.shape, o.d...]
  transfers between devices with their start and end apart: 18 -> 19, of which waited for: 9 -> 11; matrix products, arithmetic and copies ran while one was open for 0% -> 0% of each run, Pallas kernels for 3% -> 6%
where the time goes in v2:
time: 50.2 us; the launch traced here: 49.9 us
  starting transfers between devices  21.9 us (44%)
  waiting for transfers between devices  15.5 us (31%)
  Pallas kernels  8.67 us (17%)
  local copies, waits for them, and re-layouts  2.27 us (5%)
  between operations  1.56 us (3%)
    ppermute x16, starting transfers between devices, swapped(): lax.ppermute(value, axis, [(source, source ^ distance) for source in rang...  14.6 us
    ppermute x16, waiting for transfers between devices, swapped(): lax.ppermute(value, axis, [(source, source ^ distance) for source in rang...  13.8 us
    pallas_call x10, Pallas kernels, vmem_call(): pl.pallas_call(kernel, out_shape=tuple((jax.ShapeDtypeStruct(o.shape, o.d...  8.67 us
    ppermute x2, starting transfers between devices, moved_along(): lax.ppermute(value, axis, [(source, source + steps) for source in range(f...  6.01 us
    ppermute x2, waiting for transfers between devices, moved_along(): lax.ppermute(value, axis, [(source, source + steps) for source in range(f...  1.73 us
    ppermute x1, starting transfers between devices, body(): d_mine = lax.ppermute(d_send, ('row', 'col'), diagonal)  1.28 us
    dynamic_slice x1, local copies, waits for them, and re-layouts, body(): lax.dynamic_slice_in_dim(object_field, mode * part, part, 0)  1.22 us
  transfers between devices with their start and end apart: 19, of which 11 were waited for; matrix products, arithmetic and copies ran while one was open for 0% of the time, Pallas kernels for 6%

profile of v2, /device:TPU:0, one launch (start us, length us, event | category | flops | bytes accessed | tf_op | source)
XLA Modules:
  0.0 49.9 jit_solution(13876265104442283454)
XLA Ops:
  0.6 0.0 copy-start
  0.6 1.2 %constant_dynamic-slice_fusion = bf16[96,2,512]{2,1,0:T(2,128)(2,1)S(1)} fusion(f32[256,2,512]{2,1,0:T(2,128)} %object_ref.1, s32[]{:T(128)S(6)} %select_n.6), kind=kLoop, calls=%fused_computation.9 | loop fusion | bytes 393220 | tf_op jit(solution)/shard_map/dynamic_slice | solution.py:400
  1.9 0.1 maximum_maximum_fusion
  2.0 1.3 %collective-permute-start.1 = (bf16[2,144,128]{2,1,0:T(8,128)(2,1)S(1)}, bf16[2,144,128]{2,1,0:T(8,128)(2,1)S(1)}, u32[]{:S(2)}, u32[]{:S(2)}) collective-permute-start(bf16[2,144,128]{2,1,0:T(8,128)(2,1)S(1)} %maximum_maximum_fusion), channel_id=1, source_target_pairs={{6,0},{10,4},{14,8},{7,1},{11,5},{15,9},{22,16},{26,20},{30,24},{2... | collective-permute-start | bytes 221192 | tf_op jit(solution)/shard_map/ppermute | solution.py:414
  3.3 1.3 %collective-permute-start = (bf16[2,96,512]{2,1,0:T(8,128)(2,1)S(1)}, bf16[2,96,512]{2,1,0:T(8,128)(2,1)S(1)}, u32[]{:S(2)}, u32[]{:S(2)}) collective-permute-start(bf16[2,96,512]{2,1,0:T(8,128)(2,1)S(1)} %bitcast.14), channel_id=1, source_target_pairs={{4,0},{8,4},{12,8},{5,1},{9,5},{13,9},{6,2},{10,6},{14,10},{7,3},{... | collective-permute-start | bytes 589832 | tf_op jit(solution)/shard_map/ppermute | solution.py:352
  4.6 0.0 copy-done
  4.6 0.2 copy.24
  4.8 0.0 copy-start.6
  4.8 0.0 copy-start.1
  4.9 2.4 %collective-permute-start.2 = (bf16[1,128,192]{2,1,0:T(8,128)(2,1)S(1)}, bf16[1,128,192]{2,1,0:T(8,128)(2,1)S(1)}, u32[]{:S(2)}, u32[]{:S(2)}) collective-permute-start(bf16[1,128,192]{2,1,0:T(8,128)(2,1)S(1)} %get-tuple-element.45), channel_id=1, source_target_pairs={{0,2},{2,0},{1,3},{3,1},{4,6},{6,4},{5,7},{7,5},{8,10},{10,8},{9,1... | collective-permute-start | bytes 147464 | tf_op jit(solution)/shard_map/ppermute | solution.py:357
  7.3 0.1 collective-permute-start.3
  7.3 3.6 %collective-permute-done.2 = bf16[1,128,192]{2,1,0:T(8,128)(2,1)S(1)} collective-permute-done((bf16[1,128,192]{2,1,0:T(8,128)(2,1)S(1)}, bf16[1,128,192]{2,1,0:T(8,128)(2,1)S(1)}, u32[]{:S(2)}, u32[]{:S(2)}) %collective-permute-start.2) | collective-permute-done | bytes 49184 | tf_op jit(solution)/shard_map/ppermute | solution.py:357
  11.0 1.3 %collective-permute-done.3 = bf16[1,128,192]{2,1,0:T(8,128)(2,1)S(1)} collective-permute-done((bf16[1,128,192]{2,1,0:T(8,128)(2,1)S(1)}, bf16[1,128,192]{2,1,0:T(8,128)(2,1)S(1)}, u32[]{:S(2)}, u32[]{:S(2)}) %collective-permute-start.3) | collective-permute-done | bytes 49184 | tf_op jit(solution)/shard_map/ppermute | solution.py:357
  12.3 0.0 collective-permute-done.1.d_mine
  12.3 0.8 %collective-permute-done.r_mine = bf16[2,96,512]{2,1,0:T(8,128)(2,1)S(1)} collective-permute-done((bf16[2,96,512]{2,1,0:T(8,128)(2,1)S(1)}, bf16[2,96,512]{2,1,0:T(8,128)(2,1)S(1)}, u32[]{:S(2)}, u32[]{:S(2)}) %collective-permute-start) | collective-permute-done | bytes 196640 | tf_op jit(solution)/shard_map/ppermute | solution.py:352
  13.1 0.0 collective-permute-start.4
  13.2 0.5 collective-permute-start.5
  13.7 0.1 collective-permute-start.6
  14.4 0.0 copy-done.1
  14.4 0.0 copy-start.2
  14.4 0.0 copy-start.5
  14.5 0.5 collective-permute-done.6.d_other
  14.9 0.0 collective-permute-done.5.x_other
  14.9 0.0 collective-permute-done.4.r_other
  14.9 0.0 copy-start.4
  14.9 0.0 copy-done.6
  15.0 0.5 copy-done.2
  15.4 0.2 copy-done.5
  15.6 0.0 copy-done.3
  15.7 0.0 copy-done.4
  15.7 4.9 %frames.1 = (f32[2,224,512]{2,1,0:T(8,128)S(1)}, f32[2,224,512]{2,1,0:T(8,128)S(1)}, f32[2,336,128]{2,1,0:T(8,128)S(1)}, f32[2,336,128]{2,1,0:T(8,128)S(1)}, f32...) custom-call(s32[4]{0:T(128)S(1)} %copy-done.3, s32[4]{0:T(128)S(1)} %copy-done.4, ...), custom_call_target="tpu_custom_call" | custom-call | flops 2147483648 | bytes 6672420 | tf_op jit(solution)/shard_map/frames/pallas_call | solution.py:43
  20.6 0.4 collective-permute-start.8
  21.0 0.1 collective-permute-start.7
  21.2 1.7 %collective-permute-done.7.rrecv = f32[2,336,128]{2,1,0:T(8,128)S(1)} collective-permute-done((f32[2,336,128]{2,1,0:T(8,128)S(1)}, f32[2,336,128]{2,1,0:T(8,128)S(1)}, u32[]{:S(2)}, u32[]{:S(2)}) %collective-permute-start.7) | collective-permute-done | bytes 344096 | tf_op jit(solution)/shard_map/ppermute | solution.py:357
  22.9 0.0 collective-permute-done.8.grecv
  22.9 0.4 collective-permute-start.9
  23.3 0.2 after_mode.1
  23.5 1.5 %collective-permute-start.10 = (s16[688,128]{1,0:T(8,128)(2,1)S(1)}, s16[688,128]{1,0:T(8,128)(2,1)S(1)}, u32[]{:S(2)}, u32[]{:S(2)}) collective-permute-start(s16[688,128]{1,0:T(8,128)(2,1)S(1)} %get-tuple-element.60), channel_id=1, source_target_pairs={{0,2},{2,0},{1,3},{3,1},{4,6},{6,4},{5,7},{7,5},{8,10},{10,8},{9,1... | collective-permute-start | bytes 528392 | tf_op jit(solution)/shard_map/ppermute | solution.py:357
  25.0 2.3 %collective-permute-start.11 = (s16[528,128]{1,0:T(8,128)(2,1)S(1)}, s16[528,128]{1,0:T(8,128)(2,1)S(1)}, u32[]{:S(2)}, u32[]{:S(2)}) collective-permute-start(s16[528,128]{1,0:T(8,128)(2,1)S(1)} %get-tuple-element.62), channel_id=1, source_target_pairs={{0,4},{4,0},{8,12},{12,8},{1,5},{5,1},{9,13},{13,9},{2,6},{6,2},{1... | collective-permute-start | bytes 405512 | tf_op jit(solution)/shard_map/ppermute | solution.py:357
  27.3 2.2 %collective-permute-start.12 = (s16[272,128]{1,0:T(8,128)(2,1)S(1)}, s16[272,128]{1,0:T(8,128)(2,1)S(1)}, u32[]{:S(2)}, u32[]{:S(2)}) collective-permute-start(s16[272,128]{1,0:T(8,128)(2,1)S(1)} %get-tuple-element.64), channel_id=1, source_target_pairs={{0,8},{4,12},{8,0},{12,4},{1,9},{5,13},{9,1},{13,5},{2,10},{6,14},... | collective-permute-start | bytes 208904 | tf_op jit(solution)/shard_map/ppermute | solution.py:357
  29.6 3.3 %collective-permute-done.12.wrecv = s16[272,128]{1,0:T(8,128)(2,1)S(1)} collective-permute-done((s16[272,128]{1,0:T(8,128)(2,1)S(1)}, s16[272,128]{1,0:T(8,128)(2,1)S(1)}, u32[]{:S(2)}, u32[]{:S(2)}) %collective-permute-start.12) | collective-permute-done | bytes 69664 | tf_op jit(solution)/shard_map/ppermute | solution.py:357
  32.9 0.0 collective-permute-done.11.grecv
  32.9 0.2 joined.1
  33.1 0.0 collective-permute-done.10.xrecv
  33.1 0.4 collective-permute-start.14
  33.5 0.0 collective-permute-done.9.lrecv
  33.5 0.2 from_left.1
  33.7 4.7 %collective-permute-start.13 = (s16[784,128]{1,0:T(8,128)(2,1)S(1)}, s16[784,128]{1,0:T(8,128)(2,1)S(1)}, u32[]{:S(2)}, u32[]{:S(2)}) collective-permute-start(s16[784,128]{1,0:T(8,128)(2,1)S(1)} %get-tuple-element.68), channel_id=1, source_target_pairs={{0,4},{4,8},{8,12},{1,5},{5,9},{9,13},{2,6},{6,10},{10,14},{3,7},{... | collective-permute-start | bytes 602120 | tf_op jit(solution)/shard_map/ppermute | solution.py:352
  38.5 0.4 collective-permute-done.14.recv
  38.9 0.2 split.1
  39.0 2.3 %collective-permute-start.16 = (s16[528,128]{1,0:T(8,128)(2,1)S(1)}, s16[528,128]{1,0:T(8,128)(2,1)S(1)}, u32[]{:S(2)}, u32[]{:S(2)}) collective-permute-start(s16[528,128]{1,0:T(8,128)(2,1)S(1)} %get-tuple-element.76), channel_id=1, source_target_pairs={{0,8},{4,12},{8,0},{12,4},{1,9},{5,13},{9,1},{13,5},{2,10},{6,14},... | collective-permute-start | bytes 405512 | tf_op jit(solution)/shard_map/ppermute | solution.py:357
  41.3 1.6 %collective-permute-start.17 = (s16[528,128]{1,0:T(8,128)(2,1)S(1)}, s16[528,128]{1,0:T(8,128)(2,1)S(1)}, u32[]{:S(2)}, u32[]{:S(2)}) collective-permute-start(s16[528,128]{1,0:T(8,128)(2,1)S(1)} %get-tuple-element.81), channel_id=1, source_target_pairs={{0,4},{4,0},{8,12},{12,8},{1,5},{5,1},{9,13},{13,9},{2,6},{6,2},{1... | collective-permute-start | bytes 405512 | tf_op jit(solution)/shard_map/ppermute | solution.py:357
  43.0 0.9 %collective-permute-done.13.rowrecv = s16[784,128]{1,0:T(8,128)(2,1)S(1)} collective-permute-done((s16[784,128]{1,0:T(8,128)(2,1)S(1)}, s16[784,128]{1,0:T(8,128)(2,1)S(1)}, u32[]{:S(2)}, u32[]{:S(2)}) %collective-permute-start.13) | collective-permute-done | bytes 200736 | tf_op jit(solution)/shard_map/ppermute | solution.py:352
  43.9 0.1 from_above.1
  43.9 0.1 collective-permute-start.15
  44.0 1.3 %collective-permute-done.15.spilled = f32[2,32,512]{2,1,0:T(8,128)S(1)} collective-permute-done((f32[2,32,512]{2,1,0:T(8,128)S(1)}, f32[2,32,512]{2,1,0:T(8,128)S(1)}, u32[]{:S(2)}, u32[]{:S(2)}) %collective-permute-start.15) | collective-permute-done | bytes 131104 | tf_op jit(solution)/shard_map/ppermute | solution.py:357
  45.4 1.1 %object.1 = f32[128,2,512]{2,1,0:T(2,128)} custom-call(f32[256,2,512]{2,1,0:T(2,128)S(1)} %copy-done, f32[2,128,512]{2,1,0:T(8,128)S(1)} %get-tuple-element.67.tile, f32[2,96,512]{2,1,0:T(8,128)S(1)} %get-tuple-element.73.rows, f32[2,32,512]{2,1,0:T(8,128)S(1)} %collective-permute-done.15.spilled, f32[8,128]{1,0:T(8,128)S(1)} %get-tuple-element.75.peak), custom_call_target="tpu_custom_call" | custom-call | bytes 2625536 | tf_op jit(solution)/shard_map/object/pallas_call | solution.py:43
  46.4 0.0 collective-permute-done.16.grecv
  46.4 0.9 %collective-permute-done.17.wrecv = s16[528,128]{1,0:T(8,128)(2,1)S(1)} collective-permute-done((s16[528,128]{1,0:T(8,128)(2,1)S(1)}, s16[528,128]{1,0:T(8,128)(2,1)S(1)}, u32[]{:S(2)}, u32[]{:S(2)}) %collective-permute-start.17) | collective-permute-done | bytes 135200 | tf_op jit(solution)/shard_map/ppermute | solution.py:357
  47.4 0.1 probe.1.step
  47.4 0.1 collective-permute-start.18
  47.5 0.9 %probe_mine.1.before_ref = f32[256,2,256]{2,1,0:T(2,128)} custom-call(f32[256,2,256]{2,1,0:T(2,128)S(1)} %copy-done.1, f32[2,128,256]{2,1,0:T(8,128)S(1)} %probe.1.step), custom_call_target="tpu_custom_call" | custom-call | bytes 1310720 | tf_op jit(solution)/shard_map/probe_mine/pallas_call | solution.py:43
  48.4 0.6 %collective-permute-done.18.step = f32[2,128,256]{2,1,0:T(8,128)S(1)} collective-permute-done((f32[2,128,256]{2,1,0:T(8,128)S(1)}, f32[2,128,256]{2,1,0:T(8,128)S(1)}, u32[]{:S(2)}, u32[]{:S(2)}) %collective-permute-start.18) | collective-permute-done | bytes 262176 | tf_op jit(solution)/shard_map/ppermute | solution.py:357
  49.1 0.9 %probe_other.1 = f32[256,2,256]{2,1,0:T(2,128)} custom-call(f32[256,2,256]{2,1,0:T(2,128)S(1)} %copy-done.1, f32[2,128,256]{2,1,0:T(8,128)S(1)} %collective-permute-done.18.step, f32[256,2,256]{2,1,0:T(2,128)} %probe_mine.1.before_ref), custom_call_target="tpu_custom_call", output_to_operand_aliasing={{}: (2, {})} | custom-call | bytes 1835008 | tf_op jit(solution)/shard_map/probe_other/pallas_call | solution.py:43
  (10 shorter events, 0.1 us)
Async XLA Ops:
  0.6 4.0 %copy-start = (f32[256,2,512]{2,1,0:T(2,128)S(1)}, f32[256,2,512]{2,1,0:T(2,128)}, u32[]{:S(2)}) copy-start(f32[256,2,512]{2,1,0:T(2,128)} %object_ref.1) | copy-start | bytes 3145732
  2.0 10.3 %collective-permute-start.1 = (bf16[2,144,128]{2,1,0:T(8,128)(2,1)S(1)}, bf16[2,144,128]{2,1,0:T(8,128)(2,1)S(1)}, u32[]{:S(2)}, u32[]{:S(2)}) collective-permute-start(bf16[2,144,128]{2,1,0:T(8,128)(2,1)S(1)} %maximum_maximum_fusion), channel_id=1, source_target_pairs={{6,0},{10,4},{14,8},{7,1},{11,5},{15,9},{22,16},{26,20},{30,24},{2... | collective-permute-start | bytes 221192 | tf_op jit(solution)/shard_map/ppermute | solution.py:414
  3.3 9.8 %collective-permute-start = (bf16[2,96,512]{2,1,0:T(8,128)(2,1)S(1)}, bf16[2,96,512]{2,1,0:T(8,128)(2,1)S(1)}, u32[]{:S(2)}, u32[]{:S(2)}) collective-permute-start(bf16[2,96,512]{2,1,0:T(8,128)(2,1)S(1)} %bitcast.14), channel_id=1, source_target_pairs={{4,0},{8,4},{12,8},{5,1},{9,5},{13,9},{6,2},{10,6},{14,10},{7,3},{... | collective-permute-start | bytes 589832 | tf_op jit(solution)/shard_map/ppermute | solution.py:352
  4.8 10.2 %copy-start.6 = (bf16[512,512]{1,0:T(8,128)(2,1)S(1)}, bf16[512,512]{1,0:T(8,128)(2,1)}, u32[]{:S(2)}) copy-start(bf16[512,512]{1,0:T(8,128)(2,1)} %constant.16.clone.plus_ref) | copy-start | bytes 1572868
  4.8 9.6 %copy-start.1 = (f32[256,2,256]{2,1,0:T(2,128)S(1)}, f32[256,2,256]{2,1,0:T(2,128)}, u32[]{:S(2)}) copy-start(f32[256,2,256]{2,1,0:T(2,128)} %probe_ref.3) | copy-start | bytes 1572868
  4.9 6.1 %collective-permute-start.2 = (bf16[1,128,192]{2,1,0:T(8,128)(2,1)S(1)}, bf16[1,128,192]{2,1,0:T(8,128)(2,1)S(1)}, u32[]{:S(2)}, u32[]{:S(2)}) collective-permute-start(bf16[1,128,192]{2,1,0:T(8,128)(2,1)S(1)} %get-tuple-element.45), channel_id=1, source_target_pairs={{0,2},{2,0},{1,3},{3,1},{4,6},{6,4},{5,7},{7,5},{8,10},{10,8},{9,1... | collective-permute-start | bytes 147464 | tf_op jit(solution)/shard_map/ppermute | solution.py:357
  7.3 5.1 %collective-permute-start.3 = (bf16[1,128,192]{2,1,0:T(8,128)(2,1)S(1)}, bf16[1,128,192]{2,1,0:T(8,128)(2,1)S(1)}, u32[]{:S(2)}, u32[]{:S(2)}) collective-permute-start(bf16[1,128,192]{2,1,0:T(8,128)(2,1)S(1)} %get-tuple-element.46), channel_id=1, source_target_pairs={{0,2},{2,0},{1,3},{3,1},{4,6},{6,4},{5,7},{7,5},{8,10},{10,8},{9,1... | collective-permute-start | bytes 147464 | tf_op jit(solution)/shard_map/ppermute | solution.py:357
  13.1 1.8 %collective-permute-start.4 = (bf16[2,96,512]{2,1,0:T(8,128)(2,1)S(1)}, bf16[2,96,512]{2,1,0:T(8,128)(2,1)S(1)}, u32[]{:S(2)}, u32[]{:S(2)}) collective-permute-start(bf16[2,96,512]{2,1,0:T(8,128)(2,1)S(1)} %collective-permute-done.r_mine), channel_id=1, source_target_pairs={{0,1},{1,0},{2,3},{3,2},{4,5},{5,4},{6,7},{7,6},{8,9},{9,8},{10,11... | collective-permute-start | bytes 589832 | tf_op jit(solution)/shard_map/ppermute | solution.py:357
  13.2 1.8 %collective-permute-start.5 = (bf16[2,128,192]{2,1,0:T(8,128)(2,1)S(1)}, bf16[2,128,192]{2,1,0:T(8,128)(2,1)S(1)}, u32[]{:S(2)}, u32[]{:S(2)}) collective-permute-start(bf16[2,128,192]{2,1,0:T(8,128)(2,1)S(1)} %constant_dynamic-update-slice_fusion.x_mine), channel_id=1, source_target_pairs={{0,1},{1,0},{2,3},{3,2},{4,5},{5,4},{6,7},{7,6},{8,9},{9,8},{10,11... | collective-permute-start | bytes 294920 | tf_op jit(solution)/shard_map/ppermute | solution.py:357
  13.7 1.3 %collective-permute-start.6 = (bf16[2,144,128]{2,1,0:T(8,128)(2,1)S(1)}, bf16[2,144,128]{2,1,0:T(8,128)(2,1)S(1)}, u32[]{:S(2)}, u32[]{:S(2)}) collective-permute-start(bf16[2,144,128]{2,1,0:T(8,128)(2,1)S(1)} %collective-permute-done.1.d_mine), channel_id=1, source_target_pairs={{0,1},{1,0},{2,3},{3,2},{4,5},{5,4},{6,7},{7,6},{8,9},{9,8},{10,11... | collective-permute-start | bytes 221192 | tf_op jit(solution)/shard_map/ppermute | solution.py:357
  14.4 1.0 %copy-start.2 = (bf16[4,256,256]{2,1,0:T(8,128)(2,1)S(1)}, bf16[4,256,256]{2,1,0:T(8,128)(2,1)}, u32[]{:S(2)}) copy-start(bf16[4,256,256]{2,1,0:T(8,128)(2,1)} %amp_ref.1) | copy-start | bytes 1572868
  14.4 1.2 %copy-start.5 = (bf16[512,512]{1,0:T(8,128)(2,1)S(1)}, bf16[512,512]{1,0:T(8,128)(2,1)}, u32[]{:S(2)}) copy-start(bf16[512,512]{1,0:T(8,128)(2,1)} %constant.17.clone.minus_ref) | copy-start | bytes 1572868
  14.9 0.7 %copy-start.3 = (s32[4]{0:T(128)S(1)}, s32[4]{0:T(128)}, u32[]{:S(2)}) copy-start(s32[4]{0:T(128)} %row_ref.1) | copy-start | bytes 52
  14.9 0.7 %copy-start.4 = (s32[4]{0:T(128)S(1)}, s32[4]{0:T(128)}, u32[]{:S(2)}) copy-start(s32[4]{0:T(128)} %col_ref.1) | copy-start | bytes 52
  20.6 2.3 %collective-permute-start.8 = (f32[3,128,256]{2,1,0:T(8,128)S(1)}, f32[3,128,256]{2,1,0:T(8,128)S(1)}, u32[]{:S(2)}, u32[]{:S(2)}) collective-permute-start(f32[3,128,256]{2,1,0:T(8,128)S(1)} %get-tuple-element.53), channel_id=1, source_target_pairs={{0,1},{1,0},{2,3},{3,2},{4,5},{5,4},{6,7},{7,6},{8,9},{9,8},{10,11... | collective-permute-start | bytes 1179656 | tf_op jit(solution)/shard_map/ppermute | solution.py:357
  21.0 1.9 %collective-permute-start.7 = (f32[2,336,128]{2,1,0:T(8,128)S(1)}, f32[2,336,128]{2,1,0:T(8,128)S(1)}, u32[]{:S(2)}, u32[]{:S(2)}) collective-permute-start(f32[2,336,128]{2,1,0:T(8,128)S(1)} %get-tuple-element.52), channel_id=1, source_target_pairs={{0,1},{1,0},{2,3},{3,2},{4,5},{5,4},{6,7},{7,6},{8,9},{9,8},{10,11... | collective-permute-start | bytes 1032200 | tf_op jit(solution)/shard_map/ppermute | solution.py:357
  22.9 10.6 %collective-permute-start.9 = (f32[2,224,512]{2,1,0:T(8,128)S(1)}, f32[2,224,512]{2,1,0:T(8,128)S(1)}, u32[]{:S(2)}, u32[]{:S(2)}) collective-permute-start(f32[2,224,512]{2,1,0:T(8,128)S(1)} %get-tuple-element.55), channel_id=1, source_target_pairs={{0,1},{1,0},{2,3},{3,2},{4,5},{5,4},{6,7},{7,6},{8,9},{9,8},{10,11... | collective-permute-start | bytes 2752520 | tf_op jit(solution)/shard_map/ppermute | solution.py:357
  23.5 9.6 %collective-permute-start.10 = (s16[688,128]{1,0:T(8,128)(2,1)S(1)}, s16[688,128]{1,0:T(8,128)(2,1)S(1)}, u32[]{:S(2)}, u32[]{:S(2)}) collective-permute-start(s16[688,128]{1,0:T(8,128)(2,1)S(1)} %get-tuple-element.60), channel_id=1, source_target_pairs={{0,2},{2,0},{1,3},{3,1},{4,6},{6,4},{5,7},{7,5},{8,10},{10,8},{9,1... | collective-permute-start | bytes 528392 | tf_op jit(solution)/shard_map/ppermute | solution.py:357
  25.0 7.9 %collective-permute-start.11 = (s16[528,128]{1,0:T(8,128)(2,1)S(1)}, s16[528,128]{1,0:T(8,128)(2,1)S(1)}, u32[]{:S(2)}, u32[]{:S(2)}) collective-permute-start(s16[528,128]{1,0:T(8,128)(2,1)S(1)} %get-tuple-element.62), channel_id=1, source_target_pairs={{0,4},{4,0},{8,12},{12,8},{1,5},{5,1},{9,13},{13,9},{2,6},{6,2},{1... | collective-permute-start | bytes 405512 | tf_op jit(solution)/shard_map/ppermute | solution.py:357
  27.3 5.6 %collective-permute-start.12 = (s16[272,128]{1,0:T(8,128)(2,1)S(1)}, s16[272,128]{1,0:T(8,128)(2,1)S(1)}, u32[]{:S(2)}, u32[]{:S(2)}) collective-permute-start(s16[272,128]{1,0:T(8,128)(2,1)S(1)} %get-tuple-element.64), channel_id=1, source_target_pairs={{0,8},{4,12},{8,0},{12,4},{1,9},{5,13},{9,1},{13,5},{2,10},{6,14},... | collective-permute-start | bytes 208904 | tf_op jit(solution)/shard_map/ppermute | solution.py:357
  33.1 5.8 %collective-permute-start.14 = (s16[784,128]{1,0:T(8,128)(2,1)S(1)}, s16[784,128]{1,0:T(8,128)(2,1)S(1)}, u32[]{:S(2)}, u32[]{:S(2)}) collective-permute-start(s16[784,128]{1,0:T(8,128)(2,1)S(1)} %get-tuple-element.70), channel_id=1, source_target_pairs={{0,2},{2,0},{1,3},{3,1},{4,6},{6,4},{5,7},{7,5},{8,10},{10,8},{9,1... | collective-permute-start | bytes 602120 | tf_op jit(solution)/shard_map/ppermute | solution.py:357
  33.7 10.1 %collective-permute-start.13 = (s16[784,128]{1,0:T(8,128)(2,1)S(1)}, s16[784,128]{1,0:T(8,128)(2,1)S(1)}, u32[]{:S(2)}, u32[]{:S(2)}) collective-permute-start(s16[784,128]{1,0:T(8,128)(2,1)S(1)} %get-tuple-element.68), channel_id=1, source_target_pairs={{0,4},{4,8},{8,12},{1,5},{5,9},{9,13},{2,6},{6,10},{10,14},{3,7},{... | collective-permute-start | bytes 602120 | tf_op jit(solution)/shard_map/ppermute | solution.py:352
  39.0 7.4 %collective-permute-start.16 = (s16[528,128]{1,0:T(8,128)(2,1)S(1)}, s16[528,128]{1,0:T(8,128)(2,1)S(1)}, u32[]{:S(2)}, u32[]{:S(2)}) collective-permute-start(s16[528,128]{1,0:T(8,128)(2,1)S(1)} %get-tuple-element.76), channel_id=1, source_target_pairs={{0,8},{4,12},{8,0},{12,4},{1,9},{5,13},{9,1},{13,5},{2,10},{6,14},... | collective-permute-start | bytes 405512 | tf_op jit(solution)/shard_map/ppermute | solution.py:357
  41.3 6.0 %collective-permute-start.17 = (s16[528,128]{1,0:T(8,128)(2,1)S(1)}, s16[528,128]{1,0:T(8,128)(2,1)S(1)}, u32[]{:S(2)}, u32[]{:S(2)}) collective-permute-start(s16[528,128]{1,0:T(8,128)(2,1)S(1)} %get-tuple-element.81), channel_id=1, source_target_pairs={{0,4},{4,0},{8,12},{12,8},{1,5},{5,1},{9,13},{13,9},{2,6},{6,2},{1... | collective-permute-start | bytes 405512 | tf_op jit(solution)/shard_map/ppermute | solution.py:357
  43.9 1.4 %collective-permute-start.15 = (f32[2,32,512]{2,1,0:T(8,128)S(1)}, f32[2,32,512]{2,1,0:T(8,128)S(1)}, u32[]{:S(2)}, u32[]{:S(2)}) collective-permute-start(f32[2,32,512]{2,1,0:T(8,128)S(1)} %get-tuple-element.74), channel_id=1, source_target_pairs={{0,1},{1,0},{2,3},{3,2},{4,5},{5,4},{6,7},{7,6},{8,9},{9,8},{10,11... | collective-permute-start | bytes 393224 | tf_op jit(solution)/shard_map/ppermute | solution.py:357
  47.4 1.6 %collective-permute-start.18 = (f32[2,128,256]{2,1,0:T(8,128)S(1)}, f32[2,128,256]{2,1,0:T(8,128)S(1)}, u32[]{:S(2)}, u32[]{:S(2)}) collective-permute-start(f32[2,128,256]{2,1,0:T(8,128)S(1)} %probe.1.step), channel_id=1, source_target_pairs={{0,1},{1,0},{2,3},{3,2},{4,5},{5,4},{6,7},{7,6},{8,9},{9,8},{10,11... | collective-permute-start | bytes 786440 | tf_op jit(solution)/shard_map/ppermute | solution.py:357

commit v3 on v2

--- a/solution.py
+++ b/solution.py
@@ -127,7 +127,7 @@
 def frames_kernel(
     row_ref, col_ref, count_ref, own_ref, r_mine, r_other, x_mine, x_other, d_mine, d_other,
     probe_ref, amp_ref, plus_ref, minus_ref,
-    lkeep_ref, lsend_ref, rkeep_ref, rsend_ref, gkeep_ref, gsend_ref, peak_ref,
+    lkeep_ref, lsend_ref, rkeep_ref, rsend_ref, gkeep_ref, gsend_ref,
     ext, patch, wave, half, field, total, grads,
 ):
     _, tile_rows, tile_cols = own_ref.shape
@@ -145,9 +145,6 @@
         for plane in range(2):
             ext[plane, rows, tile_cols:] = unfolded(diagonal[plane].astype(F32)).astype(BF16)
         ext[:, pl.ds(pl.multiple_of(who * mid, mid), mid), tile_cols : tile_cols + right.shape[2]] = right[...]
-
-    power = probe_ref[0] * probe_ref[0] + probe_ref[1] * probe_ref[1]
-    peak_ref[...] = jnp.broadcast_to(jnp.max(power, keepdims=True), peak_ref.shape) + EPSILON
 
     total[...] = jnp.zeros(total.shape, F32)
     grads[...] = jnp.zeros(grads.shape, F32)
@@ -298,11 +295,12 @@
         spill_ref[plane] = got[plane][:over] * came
 
 
-def object_kernel(object_ref, tile, rows, spilled, peak, out_ref):
+def object_kernel(object_ref, tile, rows, spilled, probe_ref, out_ref):
     mode = lax.axis_index("mode")
     mid, part = tile.shape[1], rows.shape[1]
     over = mid - part
-    scale = 1.0 / peak[0:1, 0:1]
+    power = probe_ref[0] * probe_ref[0] + probe_ref[1] * probe_ref[1]
+    scale = 1.0 / (jnp.max(power, keepdims=True) + EPSILON)
     for who in range(2):
 
         @pl.when(mode == who)
@@ -368,7 +366,7 @@
     g_shape = shape((3, frame // 2, frame), F32)
     return vmem_call(
         frames_kernel,
-        (l_shape, l_shape, r_shape, r_shape, g_shape, g_shape, shape((8, LANES), F32)),
+        (l_shape, l_shape, r_shape, r_shape, g_shape, g_shape),
         row_offset, col_offset, counts, own, *pieces, probe, amplitudes, plus, minus,
         smem=3,
         scratch=[
@@ -420,7 +418,7 @@
     probe = jnp.transpose(probe_field, (1, 0, 2))
 
     pieces = (r_mine, r_other, x_mine, x_other, d_mine, d_other)
-    lkeep, lsend, rkeep, rsend, gkeep, gsend, peak = frames(
+    lkeep, lsend, rkeep, rsend, gkeep, gsend = frames(
         row_offset, col_offset, counts, own, pieces, probe, amplitudes, plus, minus
     )
     held = mid + part
@@ -466,7 +464,7 @@
     )
     spilled = swapped(spill, "mode", 1)
     (object_new,) = vmem_call(
-        object_kernel, (shape((mid, 2, tile_cols), F32),), object_field, tile, rows, spilled, peak, name="object"
+        object_kernel, (shape((mid, 2, tile_cols), F32),), object_field, tile, rows, spilled, probe, name="object"
     )
     object_new, gother = lax.optimization_barrier((object_new, gother))
     (step,) = vmem_call(probe_kernel, (shape((2, quarter, frame), F32),), g, gother, w, wother, name="probe")

time: 50.2 us -> 50.1 us (level)
  no operation moved by 1% of the time
where the time goes in v3:
time: 50.1 us; the launch traced here: 49.8 us
  starting transfers between devices  22 us (44%)
  waiting for transfers between devices  15.2 us (30%)
  Pallas kernels  8.7 us (17%)
  local copies, waits for them, and re-layouts  2.27 us (5%)
  between operations  1.56 us (3%)
    ppermute x16, starting transfers between devices, swapped(): lax.ppermute(value, axis, [(source, source ^ distance) for source in rang...  14.8 us
    ppermute x16, waiting for transfers between devices, swapped(): lax.ppermute(value, axis, [(source, source ^ distance) for source in rang...  13.5 us
    pallas_call x10, Pallas kernels, vmem_call(): pl.pallas_call(kernel, out_shape=tuple((jax.ShapeDtypeStruct(o.shape, o.d...  8.7 us
    ppermute x2, starting transfers between devices, moved_along(): lax.ppermute(value, axis, [(source, source + steps) for source in range(f...  5.97 us
    ppermute x2, waiting for transfers between devices, moved_along(): lax.ppermute(value, axis, [(source, source + steps) for source in range(f...  1.69 us
    ppermute x1, starting transfers between devices, body(): d_mine = lax.ppermute(d_send, ('row', 'col'), diagonal)  1.28 us
    dynamic_slice x1, local copies, waits for them, and re-layouts, body(): lax.dynamic_slice_in_dim(object_field, mode * part, part, 0)  1.22 us
  transfers between devices with their start and end apart: 19, of which 11 were waited for; matrix products, arithmetic and copies ran while one was open for 0% of the time, Pallas kernels for 6%

profile of v3, /device:TPU:0, one launch (start us, length us, event | category | flops | bytes accessed | tf_op | source)
XLA Modules:
  0.0 49.8 jit_solution(12758807967982313706)
XLA Ops:
  0.6 0.0 copy-start
  0.6 1.2 %constant_dynamic-slice_fusion = bf16[96,2,512]{2,1,0:T(2,128)(2,1)S(1)} fusion(f32[256,2,512]{2,1,0:T(2,128)} %object_ref.1, s32[]{:T(128)S(6)} %select_n.6), kind=kLoop, calls=%fused_computation.9 | loop fusion | bytes 393220 | tf_op jit(solution)/shard_map/dynamic_slice | solution.py:398
  1.9 0.1 maximum_maximum_fusion
  2.0 1.3 %collective-permute-start.1 = (bf16[2,144,128]{2,1,0:T(8,128)(2,1)S(1)}, bf16[2,144,128]{2,1,0:T(8,128)(2,1)S(1)}, u32[]{:S(2)}, u32[]{:S(2)}) collective-permute-start(bf16[2,144,128]{2,1,0:T(8,128)(2,1)S(1)} %maximum_maximum_fusion), channel_id=1, source_target_pairs={{6,0},{10,4},{14,8},{7,1},{11,5},{15,9},{22,16},{26,20},{30,24},{2... | collective-permute-start | bytes 221192 | tf_op jit(solution)/shard_map/ppermute | solution.py:412
  3.3 1.3 %collective-permute-start = (bf16[2,96,512]{2,1,0:T(8,128)(2,1)S(1)}, bf16[2,96,512]{2,1,0:T(8,128)(2,1)S(1)}, u32[]{:S(2)}, u32[]{:S(2)}) collective-permute-start(bf16[2,96,512]{2,1,0:T(8,128)(2,1)S(1)} %bitcast.15), channel_id=1, source_target_pairs={{4,0},{8,4},{12,8},{5,1},{9,5},{13,9},{6,2},{10,6},{14,10},{7,3},{... | collective-permute-start | bytes 589832 | tf_op jit(solution)/shard_map/ppermute | solution.py:350
  4.6 0.0 copy-done
  4.6 0.2 copy.24
  4.8 0.0 copy-start.6
  4.8 0.0 copy-start.1
  4.9 2.4 %collective-permute-start.2 = (bf16[1,128,192]{2,1,0:T(8,128)(2,1)S(1)}, bf16[1,128,192]{2,1,0:T(8,128)(2,1)S(1)}, u32[]{:S(2)}, u32[]{:S(2)}) collective-permute-start(bf16[1,128,192]{2,1,0:T(8,128)(2,1)S(1)} %get-tuple-element.44), channel_id=1, source_target_pairs={{0,2},{2,0},{1,3},{3,1},{4,6},{6,4},{5,7},{7,5},{8,10},{10,8},{9,1... | collective-permute-start | bytes 147464 | tf_op jit(solution)/shard_map/ppermute | solution.py:355
  7.3 0.1 collective-permute-start.3
  7.3 3.6 %collective-permute-done.2 = bf16[1,128,192]{2,1,0:T(8,128)(2,1)S(1)} collective-permute-done((bf16[1,128,192]{2,1,0:T(8,128)(2,1)S(1)}, bf16[1,128,192]{2,1,0:T(8,128)(2,1)S(1)}, u32[]{:S(2)}, u32[]{:S(2)}) %collective-permute-start.2) | collective-permute-done | bytes 49184 | tf_op jit(solution)/shard_map/ppermute | solution.py:355
  11.0 1.3 %collective-permute-done.3 = bf16[1,128,192]{2,1,0:T(8,128)(2,1)S(1)} collective-permute-done((bf16[1,128,192]{2,1,0:T(8,128)(2,1)S(1)}, bf16[1,128,192]{2,1,0:T(8,128)(2,1)S(1)}, u32[]{:S(2)}, u32[]{:S(2)}) %collective-permute-start.3) | collective-permute-done | bytes 49184 | tf_op jit(solution)/shard_map/ppermute | solution.py:355
  12.3 0.0 collective-permute-done.1.d_mine
  12.3 0.8 %collective-permute-done.r_mine = bf16[2,96,512]{2,1,0:T(8,128)(2,1)S(1)} collective-permute-done((bf16[2,96,512]{2,1,0:T(8,128)(2,1)S(1)}, bf16[2,96,512]{2,1,0:T(8,128)(2,1)S(1)}, u32[]{:S(2)}, u32[]{:S(2)}) %collective-permute-start) | collective-permute-done | bytes 196640 | tf_op jit(solution)/shard_map/ppermute | solution.py:350
  13.1 0.0 collective-permute-start.4
  13.2 0.5 collective-permute-start.5
  13.7 0.1 collective-permute-start.6
  14.4 0.0 copy-done.1
  14.4 0.0 copy-start.2
  14.4 0.0 copy-start.5
  14.5 0.5 collective-permute-done.6.d_other
  14.9 0.0 collective-permute-done.5.x_other
  14.9 0.0 collective-permute-done.4.r_other
  14.9 0.0 copy-start.4
  14.9 0.0 copy-done.6
  15.0 0.5 copy-done.2
  15.4 0.2 copy-done.5
  15.6 0.0 copy-done.3
  15.7 0.0 copy-done.4
  15.7 4.8 %frames.1 = (f32[2,224,512]{2,1,0:T(8,128)S(1)}, f32[2,224,512]{2,1,0:T(8,128)S(1)}, f32[2,336,128]{2,1,0:T(8,128)S(1)}, f32[2,336,128]{2,1,0:T(8,128)S(1)}, f32...) custom-call(s32[4]{0:T(128)S(1)} %copy-done.3, s32[4]{0:T(128)S(1)} %copy-done.4, s32[1]{0:T(128)S(6)} %copy.27.count_ref, ...), custom_call_target="tpu_custom_call" | custom-call | flops 2147483648 | bytes 6668324 | tf_op jit(solution)/shard_map/frames/pallas_call | solution.py:43
  20.5 0.4 collective-permute-start.8
  20.9 0.2 collective-permute-start.7
  21.1 1.7 %collective-permute-done.7.rrecv = f32[2,336,128]{2,1,0:T(8,128)S(1)} collective-permute-done((f32[2,336,128]{2,1,0:T(8,128)S(1)}, f32[2,336,128]{2,1,0:T(8,128)S(1)}, u32[]{:S(2)}, u32[]{:S(2)}) %collective-permute-start.7) | collective-permute-done | bytes 344096 | tf_op jit(solution)/shard_map/ppermute | solution.py:355
  22.8 0.0 collective-permute-done.8.grecv
  22.8 0.3 collective-permute-start.9
  23.1 0.2 after_mode.1
  23.4 1.5 %collective-permute-start.10 = (s16[688,128]{1,0:T(8,128)(2,1)S(1)}, s16[688,128]{1,0:T(8,128)(2,1)S(1)}, u32[]{:S(2)}, u32[]{:S(2)}) collective-permute-start(s16[688,128]{1,0:T(8,128)(2,1)S(1)} %get-tuple-element.59), channel_id=1, source_target_pairs={{0,2},{2,0},{1,3},{3,1},{4,6},{6,4},{5,7},{7,5},{8,10},{10,8},{9,1... | collective-permute-start | bytes 528392 | tf_op jit(solution)/shard_map/ppermute | solution.py:355
  24.9 2.4 %collective-permute-start.11 = (s16[528,128]{1,0:T(8,128)(2,1)S(1)}, s16[528,128]{1,0:T(8,128)(2,1)S(1)}, u32[]{:S(2)}, u32[]{:S(2)}) collective-permute-start(s16[528,128]{1,0:T(8,128)(2,1)S(1)} %get-tuple-element.61), channel_id=1, source_target_pairs={{0,4},{4,0},{8,12},{12,8},{1,5},{5,1},{9,13},{13,9},{2,6},{6,2},{1... | collective-permute-start | bytes 405512 | tf_op jit(solution)/shard_map/ppermute | solution.py:355
  27.3 2.2 %collective-permute-start.12 = (s16[272,128]{1,0:T(8,128)(2,1)S(1)}, s16[272,128]{1,0:T(8,128)(2,1)S(1)}, u32[]{:S(2)}, u32[]{:S(2)}) collective-permute-start(s16[272,128]{1,0:T(8,128)(2,1)S(1)} %get-tuple-element.63), channel_id=1, source_target_pairs={{0,8},{4,12},{8,0},{12,4},{1,9},{5,13},{9,1},{13,5},{2,10},{6,14},... | collective-permute-start | bytes 208904 | tf_op jit(solution)/shard_map/ppermute | solution.py:355
  29.5 3.2 %collective-permute-done.12.wrecv = s16[272,128]{1,0:T(8,128)(2,1)S(1)} collective-permute-done((s16[272,128]{1,0:T(8,128)(2,1)S(1)}, s16[272,128]{1,0:T(8,128)(2,1)S(1)}, u32[]{:S(2)}, u32[]{:S(2)}) %collective-permute-start.12) | collective-permute-done | bytes 69664 | tf_op jit(solution)/shard_map/ppermute | solution.py:355
  32.8 0.0 collective-permute-done.11.grecv
  32.8 0.2 joined.1
  32.9 0.0 collective-permute-done.10.xrecv
  32.9 0.5 collective-permute-start.14
  33.4 0.0 collective-permute-done.9.lrecv
  33.4 0.2 from_left.1
  33.7 4.7 %collective-permute-start.13 = (s16[784,128]{1,0:T(8,128)(2,1)S(1)}, s16[784,128]{1,0:T(8,128)(2,1)S(1)}, u32[]{:S(2)}, u32[]{:S(2)}) collective-permute-start(s16[784,128]{1,0:T(8,128)(2,1)S(1)} %get-tuple-element.67), channel_id=1, source_target_pairs={{0,4},{4,8},{8,12},{1,5},{5,9},{9,13},{2,6},{6,10},{10,14},{3,7},{... | collective-permute-start | bytes 602120 | tf_op jit(solution)/shard_map/ppermute | solution.py:350
  38.4 0.4 collective-permute-done.14.recv
  38.7 0.2 split.1
  38.9 2.4 %collective-permute-start.16 = (s16[528,128]{1,0:T(8,128)(2,1)S(1)}, s16[528,128]{1,0:T(8,128)(2,1)S(1)}, u32[]{:S(2)}, u32[]{:S(2)}) collective-permute-start(s16[528,128]{1,0:T(8,128)(2,1)S(1)} %get-tuple-element.74), channel_id=1, source_target_pairs={{0,8},{4,12},{8,0},{12,4},{1,9},{5,13},{9,1},{13,5},{2,10},{6,14},... | collective-permute-start | bytes 405512 | tf_op jit(solution)/shard_map/ppermute | solution.py:355
  41.3 1.6 %collective-permute-start.17 = (s16[528,128]{1,0:T(8,128)(2,1)S(1)}, s16[528,128]{1,0:T(8,128)(2,1)S(1)}, u32[]{:S(2)}, u32[]{:S(2)}) collective-permute-start(s16[528,128]{1,0:T(8,128)(2,1)S(1)} %get-tuple-element.79), channel_id=1, source_target_pairs={{0,4},{4,0},{8,12},{12,8},{1,5},{5,1},{9,13},{13,9},{2,6},{6,2},{1... | collective-permute-start | bytes 405512 | tf_op jit(solution)/shard_map/ppermute | solution.py:355
  42.9 0.9 %collective-permute-done.13.rowrecv = s16[784,128]{1,0:T(8,128)(2,1)S(1)} collective-permute-done((s16[784,128]{1,0:T(8,128)(2,1)S(1)}, s16[784,128]{1,0:T(8,128)(2,1)S(1)}, u32[]{:S(2)}, u32[]{:S(2)}) %collective-permute-start.13) | collective-permute-done | bytes 200736 | tf_op jit(solution)/shard_map/ppermute | solution.py:350
  43.8 0.1 from_above.1
  43.8 0.1 collective-permute-start.15
  43.9 1.3 %collective-permute-done.15.spilled = f32[2,32,512]{2,1,0:T(8,128)S(1)} collective-permute-done((f32[2,32,512]{2,1,0:T(8,128)S(1)}, f32[2,32,512]{2,1,0:T(8,128)S(1)}, u32[]{:S(2)}, u32[]{:S(2)}) %collective-permute-start.15) | collective-permute-done | bytes 131104 | tf_op jit(solution)/shard_map/ppermute | solution.py:355
  45.2 1.2 %object.1 = f32[128,2,512]{2,1,0:T(2,128)} custom-call(f32[256,2,512]{2,1,0:T(2,128)S(1)} %copy-done, f32[2,128,512]{2,1,0:T(8,128)S(1)} %get-tuple-element.66.tile, f32[2,96,512]{2,1,0:T(8,128)S(1)} %get-tuple-element.72.rows, f32[2,32,512]{2,1,0:T(8,128)S(1)} %collective-permute-done.15.spilled, f32[2,256,256]{2,1,0:T(8,128)S(1)} %bitcast.11), custom_call_target="tpu_custom_call" | custom-call | bytes 3145728 | tf_op jit(solution)/shard_map/object/pallas_call | solution.py:43
  46.5 0.0 collective-permute-done.16.grecv
  46.5 0.8 %collective-permute-done.17.wrecv = s16[528,128]{1,0:T(8,128)(2,1)S(1)} collective-permute-done((s16[528,128]{1,0:T(8,128)(2,1)S(1)}, s16[528,128]{1,0:T(8,128)(2,1)S(1)}, u32[]{:S(2)}, u32[]{:S(2)}) %collective-permute-start.17) | collective-permute-done | bytes 135200 | tf_op jit(solution)/shard_map/ppermute | solution.py:355
  47.3 0.1 probe.1.step
  47.3 0.1 collective-permute-start.18
  47.4 0.9 %probe_mine.1.before_ref = f32[256,2,256]{2,1,0:T(2,128)} custom-call(f32[256,2,256]{2,1,0:T(2,128)S(1)} %copy-done.1, f32[2,128,256]{2,1,0:T(8,128)S(1)} %probe.1.step), custom_call_target="tpu_custom_call" | custom-call | bytes 1310720 | tf_op jit(solution)/shard_map/probe_mine/pallas_call | solution.py:43
  48.3 0.6 %collective-permute-done.18.step = f32[2,128,256]{2,1,0:T(8,128)S(1)} collective-permute-done((f32[2,128,256]{2,1,0:T(8,128)S(1)}, f32[2,128,256]{2,1,0:T(8,128)S(1)}, u32[]{:S(2)}, u32[]{:S(2)}) %collective-permute-start.18) | collective-permute-done | bytes 262176 | tf_op jit(solution)/shard_map/ppermute | solution.py:355
  48.9 0.9 %probe_other.1 = f32[256,2,256]{2,1,0:T(2,128)} custom-call(f32[256,2,256]{2,1,0:T(2,128)S(1)} %copy-done.1, f32[2,128,256]{2,1,0:T(8,128)S(1)} %collective-permute-done.18.step, f32[256,2,256]{2,1,0:T(2,128)} %probe_mine.1.before_ref), custom_call_target="tpu_custom_call", output_to_operand_aliasing={{}: (2, {})} | custom-call | bytes 1835008 | tf_op jit(solution)/shard_map/probe_other/pallas_call | solution.py:43
  (10 shorter events, 0.1 us)
Async XLA Ops:
  0.6 4.0 %copy-start = (f32[256,2,512]{2,1,0:T(2,128)S(1)}, f32[256,2,512]{2,1,0:T(2,128)}, u32[]{:S(2)}) copy-start(f32[256,2,512]{2,1,0:T(2,128)} %object_ref.1) | copy-start | bytes 3145732
  2.0 10.3 %collective-permute-start.1 = (bf16[2,144,128]{2,1,0:T(8,128)(2,1)S(1)}, bf16[2,144,128]{2,1,0:T(8,128)(2,1)S(1)}, u32[]{:S(2)}, u32[]{:S(2)}) collective-permute-start(bf16[2,144,128]{2,1,0:T(8,128)(2,1)S(1)} %maximum_maximum_fusion), channel_id=1, source_target_pairs={{6,0},{10,4},{14,8},{7,1},{11,5},{15,9},{22,16},{26,20},{30,24},{2... | collective-permute-start | bytes 221192 | tf_op jit(solution)/shard_map/ppermute | solution.py:412
  3.3 9.8 %collective-permute-start = (bf16[2,96,512]{2,1,0:T(8,128)(2,1)S(1)}, bf16[2,96,512]{2,1,0:T(8,128)(2,1)S(1)}, u32[]{:S(2)}, u32[]{:S(2)}) collective-permute-start(bf16[2,96,512]{2,1,0:T(8,128)(2,1)S(1)} %bitcast.15), channel_id=1, source_target_pairs={{4,0},{8,4},{12,8},{5,1},{9,5},{13,9},{6,2},{10,6},{14,10},{7,3},{... | collective-permute-start | bytes 589832 | tf_op jit(solution)/shard_map/ppermute | solution.py:350
  4.8 10.2 %copy-start.6 = (bf16[512,512]{1,0:T(8,128)(2,1)S(1)}, bf16[512,512]{1,0:T(8,128)(2,1)}, u32[]{:S(2)}) copy-start(bf16[512,512]{1,0:T(8,128)(2,1)} %constant.16.clone.plus_ref) | copy-start | bytes 1572868
  4.8 9.6 %copy-start.1 = (f32[256,2,256]{2,1,0:T(2,128)S(1)}, f32[256,2,256]{2,1,0:T(2,128)}, u32[]{:S(2)}) copy-start(f32[256,2,256]{2,1,0:T(2,128)} %probe_ref.3) | copy-start | bytes 1572868
  4.9 6.1 %collective-permute-start.2 = (bf16[1,128,192]{2,1,0:T(8,128)(2,1)S(1)}, bf16[1,128,192]{2,1,0:T(8,128)(2,1)S(1)}, u32[]{:S(2)}, u32[]{:S(2)}) collective-permute-start(bf16[1,128,192]{2,1,0:T(8,128)(2,1)S(1)} %get-tuple-element.44), channel_id=1, source_target_pairs={{0,2},{2,0},{1,3},{3,1},{4,6},{6,4},{5,7},{7,5},{8,10},{10,8},{9,1... | collective-permute-start | bytes 147464 | tf_op jit(solution)/shard_map/ppermute | solution.py:355
  7.3 5.1 %collective-permute-start.3 = (bf16[1,128,192]{2,1,0:T(8,128)(2,1)S(1)}, bf16[1,128,192]{2,1,0:T(8,128)(2,1)S(1)}, u32[]{:S(2)}, u32[]{:S(2)}) collective-permute-start(bf16[1,128,192]{2,1,0:T(8,128)(2,1)S(1)} %get-tuple-element.45), channel_id=1, source_target_pairs={{0,2},{2,0},{1,3},{3,1},{4,6},{6,4},{5,7},{7,5},{8,10},{10,8},{9,1... | collective-permute-start | bytes 147464 | tf_op jit(solution)/shard_map/ppermute | solution.py:355
  13.1 1.8 %collective-permute-start.4 = (bf16[2,96,512]{2,1,0:T(8,128)(2,1)S(1)}, bf16[2,96,512]{2,1,0:T(8,128)(2,1)S(1)}, u32[]{:S(2)}, u32[]{:S(2)}) collective-permute-start(bf16[2,96,512]{2,1,0:T(8,128)(2,1)S(1)} %collective-permute-done.r_mine), channel_id=1, source_target_pairs={{0,1},{1,0},{2,3},{3,2},{4,5},{5,4},{6,7},{7,6},{8,9},{9,8},{10,11... | collective-permute-start | bytes 589832 | tf_op jit(solution)/shard_map/ppermute | solution.py:355
  13.2 1.8 %collective-permute-start.5 = (bf16[2,128,192]{2,1,0:T(8,128)(2,1)S(1)}, bf16[2,128,192]{2,1,0:T(8,128)(2,1)S(1)}, u32[]{:S(2)}, u32[]{:S(2)}) collective-permute-start(bf16[2,128,192]{2,1,0:T(8,128)(2,1)S(1)} %constant_dynamic-update-slice_fusion.x_mine), channel_id=1, source_target_pairs={{0,1},{1,0},{2,3},{3,2},{4,5},{5,4},{6,7},{7,6},{8,9},{9,8},{10,11... | collective-permute-start | bytes 294920 | tf_op jit(solution)/shard_map/ppermute | solution.py:355
  13.7 1.3 %collective-permute-start.6 = (bf16[2,144,128]{2,1,0:T(8,128)(2,1)S(1)}, bf16[2,144,128]{2,1,0:T(8,128)(2,1)S(1)}, u32[]{:S(2)}, u32[]{:S(2)}) collective-permute-start(bf16[2,144,128]{2,1,0:T(8,128)(2,1)S(1)} %collective-permute-done.1.d_mine), channel_id=1, source_target_pairs={{0,1},{1,0},{2,3},{3,2},{4,5},{5,4},{6,7},{7,6},{8,9},{9,8},{10,11... | collective-permute-start | bytes 221192 | tf_op jit(solution)/shard_map/ppermute | solution.py:355
  14.4 1.0 %copy-start.2 = (bf16[4,256,256]{2,1,0:T(8,128)(2,1)S(1)}, bf16[4,256,256]{2,1,0:T(8,128)(2,1)}, u32[]{:S(2)}) copy-start(bf16[4,256,256]{2,1,0:T(8,128)(2,1)} %amp_ref.1) | copy-start | bytes 1572868
  14.4 1.2 %copy-start.5 = (bf16[512,512]{1,0:T(8,128)(2,1)S(1)}, bf16[512,512]{1,0:T(8,128)(2,1)}, u32[]{:S(2)}) copy-start(bf16[512,512]{1,0:T(8,128)(2,1)} %constant.17.clone.minus_ref) | copy-start | bytes 1572868
  14.9 0.7 %copy-start.3 = (s32[4]{0:T(128)S(1)}, s32[4]{0:T(128)}, u32[]{:S(2)}) copy-start(s32[4]{0:T(128)} %row_ref.1) | copy-start | bytes 52
  14.9 0.7 %copy-start.4 = (s32[4]{0:T(128)S(1)}, s32[4]{0:T(128)}, u32[]{:S(2)}) copy-start(s32[4]{0:T(128)} %col_ref.1) | copy-start | bytes 52
  20.5 2.3 %collective-permute-start.8 = (f32[3,128,256]{2,1,0:T(8,128)S(1)}, f32[3,128,256]{2,1,0:T(8,128)S(1)}, u32[]{:S(2)}, u32[]{:S(2)}) collective-permute-start(f32[3,128,256]{2,1,0:T(8,128)S(1)} %get-tuple-element.52), channel_id=1, source_target_pairs={{0,1},{1,0},{2,3},{3,2},{4,5},{5,4},{6,7},{7,6},{8,9},{9,8},{10,11... | collective-permute-start | bytes 1179656 | tf_op jit(solution)/shard_map/ppermute | solution.py:355
  20.9 1.9 %collective-permute-start.7 = (f32[2,336,128]{2,1,0:T(8,128)S(1)}, f32[2,336,128]{2,1,0:T(8,128)S(1)}, u32[]{:S(2)}, u32[]{:S(2)}) collective-permute-start(f32[2,336,128]{2,1,0:T(8,128)S(1)} %get-tuple-element.51), channel_id=1, source_target_pairs={{0,1},{1,0},{2,3},{3,2},{4,5},{5,4},{6,7},{7,6},{8,9},{9,8},{10,11... | collective-permute-start | bytes 1032200 | tf_op jit(solution)/shard_map/ppermute | solution.py:355
  22.8 10.6 %collective-permute-start.9 = (f32[2,224,512]{2,1,0:T(8,128)S(1)}, f32[2,224,512]{2,1,0:T(8,128)S(1)}, u32[]{:S(2)}, u32[]{:S(2)}) collective-permute-start(f32[2,224,512]{2,1,0:T(8,128)S(1)} %get-tuple-element.54), channel_id=1, source_target_pairs={{0,1},{1,0},{2,3},{3,2},{4,5},{5,4},{6,7},{7,6},{8,9},{9,8},{10,11... | collective-permute-start | bytes 2752520 | tf_op jit(solution)/shard_map/ppermute | solution.py:355
  23.4 9.6 %collective-permute-start.10 = (s16[688,128]{1,0:T(8,128)(2,1)S(1)}, s16[688,128]{1,0:T(8,128)(2,1)S(1)}, u32[]{:S(2)}, u32[]{:S(2)}) collective-permute-start(s16[688,128]{1,0:T(8,128)(2,1)S(1)} %get-tuple-element.59), channel_id=1, source_target_pairs={{0,2},{2,0},{1,3},{3,1},{4,6},{6,4},{5,7},{7,5},{8,10},{10,8},{9,1... | collective-permute-start | bytes 528392 | tf_op jit(solution)/shard_map/ppermute | solution.py:355
  24.9 7.9 %collective-permute-start.11 = (s16[528,128]{1,0:T(8,128)(2,1)S(1)}, s16[528,128]{1,0:T(8,128)(2,1)S(1)}, u32[]{:S(2)}, u32[]{:S(2)}) collective-permute-start(s16[528,128]{1,0:T(8,128)(2,1)S(1)} %get-tuple-element.61), channel_id=1, source_target_pairs={{0,4},{4,0},{8,12},{12,8},{1,5},{5,1},{9,13},{13,9},{2,6},{6,2},{1... | collective-permute-start | bytes 405512 | tf_op jit(solution)/shard_map/ppermute | solution.py:355
  27.3 5.5 %collective-permute-start.12 = (s16[272,128]{1,0:T(8,128)(2,1)S(1)}, s16[272,128]{1,0:T(8,128)(2,1)S(1)}, u32[]{:S(2)}, u32[]{:S(2)}) collective-permute-start(s16[272,128]{1,0:T(8,128)(2,1)S(1)} %get-tuple-element.63), channel_id=1, source_target_pairs={{0,8},{4,12},{8,0},{12,4},{1,9},{5,13},{9,1},{13,5},{2,10},{6,14},... | collective-permute-start | bytes 208904 | tf_op jit(solution)/shard_map/ppermute | solution.py:355
  32.9 5.8 %collective-permute-start.14 = (s16[784,128]{1,0:T(8,128)(2,1)S(1)}, s16[784,128]{1,0:T(8,128)(2,1)S(1)}, u32[]{:S(2)}, u32[]{:S(2)}) collective-permute-start(s16[784,128]{1,0:T(8,128)(2,1)S(1)} %get-tuple-element.69), channel_id=1, source_target_pairs={{0,2},{2,0},{1,3},{3,1},{4,6},{6,4},{5,7},{7,5},{8,10},{10,8},{9,1... | collective-permute-start | bytes 602120 | tf_op jit(solution)/shard_map/ppermute | solution.py:355
  33.7 10.1 %collective-permute-start.13 = (s16[784,128]{1,0:T(8,128)(2,1)S(1)}, s16[784,128]{1,0:T(8,128)(2,1)S(1)}, u32[]{:S(2)}, u32[]{:S(2)}) collective-permute-start(s16[784,128]{1,0:T(8,128)(2,1)S(1)} %get-tuple-element.67), channel_id=1, source_target_pairs={{0,4},{4,8},{8,12},{1,5},{5,9},{9,13},{2,6},{6,10},{10,14},{3,7},{... | collective-permute-start | bytes 602120 | tf_op jit(solution)/shard_map/ppermute | solution.py:350
  38.9 7.6 %collective-permute-start.16 = (s16[528,128]{1,0:T(8,128)(2,1)S(1)}, s16[528,128]{1,0:T(8,128)(2,1)S(1)}, u32[]{:S(2)}, u32[]{:S(2)}) collective-permute-start(s16[528,128]{1,0:T(8,128)(2,1)S(1)} %get-tuple-element.74), channel_id=1, source_target_pairs={{0,8},{4,12},{8,0},{12,4},{1,9},{5,13},{9,1},{13,5},{2,10},{6,14},... | collective-permute-start | bytes 405512 | tf_op jit(solution)/shard_map/ppermute | solution.py:355
  41.3 6.0 %collective-permute-start.17 = (s16[528,128]{1,0:T(8,128)(2,1)S(1)}, s16[528,128]{1,0:T(8,128)(2,1)S(1)}, u32[]{:S(2)}, u32[]{:S(2)}) collective-permute-start(s16[528,128]{1,0:T(8,128)(2,1)S(1)} %get-tuple-element.79), channel_id=1, source_target_pairs={{0,4},{4,0},{8,12},{12,8},{1,5},{5,1},{9,13},{13,9},{2,6},{6,2},{1... | collective-permute-start | bytes 405512 | tf_op jit(solution)/shard_map/ppermute | solution.py:355
  43.8 1.4 %collective-permute-start.15 = (f32[2,32,512]{2,1,0:T(8,128)S(1)}, f32[2,32,512]{2,1,0:T(8,128)S(1)}, u32[]{:S(2)}, u32[]{:S(2)}) collective-permute-start(f32[2,32,512]{2,1,0:T(8,128)S(1)} %get-tuple-element.73), channel_id=1, source_target_pairs={{0,1},{1,0},{2,3},{3,2},{4,5},{5,4},{6,7},{7,6},{8,9},{9,8},{10,11... | collective-permute-start | bytes 393224 | tf_op jit(solution)/shard_map/ppermute | solution.py:355
  47.3 1.6 %collective-permute-start.18 = (f32[2,128,256]{2,1,0:T(8,128)S(1)}, f32[2,128,256]{2,1,0:T(8,128)S(1)}, u32[]{:S(2)}, u32[]{:S(2)}) collective-permute-start(f32[2,128,256]{2,1,0:T(8,128)S(1)} %probe.1.step), channel_id=1, source_target_pairs={{0,1},{1,0},{2,3},{3,2},{4,5},{5,4},{6,7},{7,6},{8,9},{9,8},{10,11... | collective-permute-start | bytes 786440 | tf_op jit(solution)/shard_map/ppermute | solution.py:355
